TPU v7x, 32 devices: a whole 2x2x4 slice. The times are simulated.
32 devices in a mesh: row: 4 (over z), col: 8 (over y, x, core).
Axes of the slice: x: 2, y: 2, z: 4, core: 2. Of those that a mesh axis runs over, the one named last changes fastest.
Arguments:
- patches: bfloat16 [24576, 1536], P(('row', 'col')), may hold values from -6 to 6
- dest: int32 [24576], P(('row', 'col')), may hold values from -1 to 511, as said below
- background: bfloat16 [1536], replicated, may hold values from -6 to 6
- conv_weight: float32 [7, 7, 1536], replicated, may hold values from -0.875 to 0.875
- conv_bias: float32 [1536], replicated, may hold values from -3 to 3
- norm_gain: float32 [1536], replicated, may hold values from 0.1 to 1.9
- norm_bias: float32 [1536], replicated, may hold values from -3 to 3
- w_in: bfloat16 [6144, 1536], P('col'), may hold values from -0.15625 to 0.15625
- b_in: bfloat16 [6144], P('col'), may hold values from -3 to 3
- w_out: bfloat16 [6144, 1536], P('col'), may hold values from -0.078125 to 0.078125
- b_out: float32 [1536], replicated, may hold values from -3 to 3
- layer_scale: float32 [1536], replicated, may hold values from 0.3 to 1.5
Outputs:
- features: bfloat16 [128, 128, 1536], P('row', 'col')
Inputs may be any that keep to these rules, and one draw needn't show every extreme that they name: `dest`: -1 marks an empty slot; no cell is named twice among all slots sent to one device; in every draw some device fills all 96 slots it sends to some device, and some device receives a patch for every one of its cells.
All inputs are finite; a program needn't handle non-finite values.
Results may differ from a plain program's by a relative error of at most 0.0046.
Values may be sent and summed in bfloat16 or wider, within the bound.
A program may use at most 128 MiB of HBM per device.

v0:
```python
import jax
import jax.numpy as jnp
from jax import lax
from jax.sharding import PartitionSpec as P

TH = 32
TW = 16


def extended(cells, sides, width):
    for axis, dim in sides:
        count = lax.axis_size(axis)
        ends = count - 1
        head = lax.slice_in_dim(cells, 0, width, axis=dim)
        tail = lax.slice_in_dim(cells, cells.shape[dim] - width, cells.shape[dim], axis=dim)
        cells = jnp.concatenate(
            [
                lax.ppermute(tail, axis, [(i, (i + 1) % count) for i in range(ends)]),
                cells,
                lax.ppermute(head, axis, [((i + 1) % count, i) for i in range(ends)]),
            ],
            axis=dim,
        )
    return cells


def expand(rows, weight_rows, bias_rows):
    pre = lax.dot_general(
        rows, weight_rows, (((1,), (1,)), ((), ())), preferred_element_type=jnp.float32
    )
    return jax.nn.gelu(pre + bias_rows.astype(jnp.float32), approximate=False).astype(jnp.bfloat16)


def local(
    patches,
    dest,
    background,
    conv_weight,
    conv_bias,
    norm_gain,
    norm_bias,
    w_in,
    b_in,
    w_out,
    b_out,
    layer_scale,
):
    cells = TH * TW
    channels = patches.shape[1]
    moved, moved_dest = (
        lax.all_to_all(patches, "col", split_axis=0, concat_axis=0, tiled=True),
        lax.all_to_all(dest, "col", split_axis=0, concat_axis=0, tiled=True),
    )
    cell_ids = jnp.arange(cells, dtype=jnp.int32)
    onehot = moved_dest[None, :] == cell_ids[:, None]
    placed = jnp.dot(onehot.astype(jnp.bfloat16), moved, preferred_element_type=jnp.float32)
    present = jnp.any(onehot, axis=1)
    grid = jnp.where(present[:, None], placed, background.astype(jnp.float32)[None, :]).astype(
        jnp.bfloat16
    )
    grid_block = grid.reshape(TH, TW, channels)
    padded = extended(grid_block, (("row", 0), ("col", 1)), 3)
    conv = jnp.zeros((TH, TW, channels), jnp.float32) + conv_bias
    for across in range(7):
        for along in range(7):
            conv = (
                conv
                + padded[across : across + TH, along : along + TW, :].astype(jnp.float32)
                * conv_weight[across, along]
            )
    mean = jnp.mean(conv, axis=-1, keepdims=True)
    centred = conv - mean
    var = jnp.mean(centred * centred, axis=-1, keepdims=True)
    normed = (centred * lax.rsqrt(var + 1e-06) * norm_gain + norm_bias).astype(jnp.bfloat16)
    flat = normed.reshape(cells, channels)
    hidden = expand(
        flat,
        lax.all_gather(w_in, "col", axis=0, tiled=True),
        lax.all_gather(b_in, "col", axis=0, tiled=True),
    )
    mixed = jnp.dot(
        hidden, lax.all_gather(w_out, "col", axis=0, tiled=True), preferred_element_type=jnp.float32
    )
    result = grid.astype(jnp.float32) + layer_scale * (mixed + b_out)
    return result.astype(jnp.bfloat16).reshape(TH, TW, channels)


def solution(mesh):
    placed = (
        P(("row", "col"), None),
        P(("row", "col")),
        P(),
        P(),
        P(),
        P(),
        P(),
        P("col", None),
        P("col"),
        P("col", None),
        P(),
        P(),
    )
    return jax.shard_map(
        local, mesh=mesh, in_specs=placed, out_specs=P("row", "col", None), check_vma=False
    )
```

profile of v0, /device:TPU:0, one launch (start us, length us, event | category | flops | bytes accessed | tf_op | source)
XLA Modules:
  0.0 269.4 jit_solution(5061967956608160431)
XLA Ops:
  6.5 0.0 all-gather.4.cloned.1.call-start
  6.5 0.7 all-gather.4.cloned.1.call-update
  7.3 0.0 copy-start.8
  7.3 0.0 all-gather.6.cloned.1.call-start
  7.3 0.7 all-gather.6.cloned.1.call-update
  8.0 0.0 copy-done.4
  8.0 0.1 all_to_all.14
  8.1 9.6 %all_to_all.21 = s32[8,96,1]{1,2,0:T(1,128)S(1)} all-to-all(s32[8,96,1]{1,2,0:T(1,128)S(1)} %bitcast.29), channel_id=1, replica_groups=mesh['row'=4,'col'=8] {'col'}, dimensions={0} | all-to-all | bytes 6144 | tf_op jit(solution)/shard_map/all_to_all | solution.py:52
  17.7 4.5 %all-to-all-start.1 = ((bf16[8,96,1536]{2,1,0:T(8,128)(2,1)}), bf16[8,96,1536]{2,1,0:T(8,128)(2,1)}, u32[]{:S(2)}, u32[]{:S(2)}) async-start(bf16[8,96,1536]{2,1,0:T(8,128)(2,1)} %bitcast.1), calls=%async_computation.1 | async-start | bytes 4718592 | tf_op jit(solution)/shard_map/all_to_all | solution.py:51
  22.2 0.5 broadcast.99
  22.7 0.7 reduce.101
  23.4 0.1 eq.15
  23.4 0.3 fusion.47
  23.7 51.9 %all-to-all-done.1 = bf16[8,96,1536]{2,1,0:T(8,128)(2,1)} async-done(((bf16[8,96,1536]{2,1,0:T(8,128)(2,1)}), bf16[8,96,1536]{2,1,0:T(8,128)(2,1)}, u32[]{:S(2)}, u32[]{:S(2)}) %all-to-all-start.1) | async-done | bytes 2359328 | tf_op jit(solution)/shard_map/all_to_all | solution.py:51
  75.6 0.0 copy-done.8
  75.6 3.1 %fusion.41 = bf16[512,1536]{1,0:T(8,128)(2,1)S(1)} fusion(bf16[768,1536]{1,0:T(8,128)(2,1)} %bitcast.2, bf16[1536]{0:T(1024)(128)(2,1)S(1)} %copy-done.8, pred[512]{0:T(512)(128)(4,1)S(1)} %fusion.47, s32[768]{0:T(1024)S(1)} %eq.15), kind=kOutput, calls=%fused_computation.54 | convolution fusion | flops 1209139200 | bytes 3938816 | tf_op jit(solution)/shard_map/dot_general | solution.py:56
  78.7 0.0 copy-start
  78.7 3.5 %collective-permute-start = (bf16[3,16,1536]{2,1,0:T(8,128)(2,1)S(1)}, bf16[3,16,1536]{2,1,0:T(8,128)(2,1)S(1)}, u32[]{:S(2)}, u32[]{:S(2)}) collective-permute-start(bf16[3,16,1536]{2,1,0:T(8,128)(2,1)S(1)} %bitcast.27), channel_id=1, source_target_pairs={{0,8},{8,16},{16,24},{1,9},{9,17},{17,25},{2,10},{10,18},{18,26},{... | collective-permute-start | bytes 442376 | tf_op jit(solution)/shard_map/ppermute | solution.py:18
  82.2 1.3 collective-permute-start.1
  83.5 0.0 copy-done.5
  83.6 8.2 %all-gather = bf16[8,1,768]{2,1,0:T(2,128)(2,1)S(1)} all-gather(bf16[1,1,768]{2,1,0:T(2,128)(2,1)S(1)} %reshape.40), channel_id=1, replica_groups=mesh['row'=4,'col'=8] {'col'}, dimensions={0}, use_global_device_ids=true | all-gather | bytes 13824 | tf_op jit(solution)/shard_map/all_gather | solution.py:79
  91.7 0.0 collective-permute-done
  91.7 0.0 collective-permute-done.1
  91.8 0.4 pad_maximum_fusion.5
  92.1 2.3 collective-permute-start.2
  94.4 1.3 collective-permute-start.3
  95.7 0.0 copy-done
  95.7 0.2 slice_reduce_fusion.46
  95.9 0.3 slice_reduce_fusion.48
  96.2 0.3 slice_reduce_fusion.47
  96.5 0.0 copy-start.1
  96.6 0.0 collective-permute-done.2
  96.6 2.3 collective-permute-done.3
  98.8 1.6 maximum_maximum_fusion
  100.5 0.0 copy-done.1
  100.5 26.2 %fusion.79 = (f32[32,16]{1,0:T(8,128)S(1)}, f32[32,16,1536]{2,1,0:T(8,128)S(1)}) fusion(f32[1536]{0:T(1024)S(1)} %get-tuple-element.52, bf16[38,19,1536]{2,1,0:T(8,128)(2,1)S(1)} %get-tuple-element.57, f32[1536]{0:T(1024)S(1)} %get-tuple-element.53, f32[1536]{0:T(1024)S(1)} %get-tuple-element.6, f32[1536]{0:T(1024)S(1)} %get-tuple-element.7, ...), kind=kLoop, calls=%fused_computation.159 | loop fusion | flops 121110016 | bytes 71383040 | tf_op jit(solution)/shard_map/reduce_sum | solution.py:71
  126.7 0.0 copy-start.2
  126.7 0.0 copy-start.3
  126.7 0.4 multiply_reduce_fusion
  127.2 0.2 copy-done.2
  127.4 0.0 copy-done.3
  127.4 0.6 add_convert_fusion
  128.0 17.3 %all-gather.4.cloned.1.call-done = bf16[6144,1536]{1,0:T(8,128)(2,1)} async-done(((bf16[768,1536]{1,0:T(8,128)(2,1)}), bf16[6144,1536]{1,0:T(8,128)(2,1)}) %all-gather.4.cloned.1.call-update) | async-done | bytes 18874384 | tf_op jit(solution)/shard_map/all_gather | solution.py:78
  145.3 39.0 %fusion.2.clone.12 = bf16[512,6144]{1,0:T(8,128)(2,1)} fusion(bf16[512,1536]{1,0:T(8,128)(2,1)S(1)} %bitcast.25, bf16[6144,1536]{1,0:T(8,128)(2,1)} %all-gather.4.cloned.1.call-done, f32[6144]{0:T(1024)S(1)} %bitcast.28), kind=kOutput, calls=%fused_computation.3.clone.clone.clone.clone.clone.clone.clone.clone.clone.clone.... | convolution fusion | flops 9871294464 | bytes 26763264 | tf_op jit(solution)/shard_map/dot_general | solution.py:28
  184.3 61.6 %all-gather.6.cloned.1.call-done = bf16[6144,1536]{1,0:T(8,128)(2,1)} async-done(((bf16[768,1536]{1,0:T(8,128)(2,1)}), bf16[6144,1536]{1,0:T(8,128)(2,1)}) %all-gather.6.cloned.1.call-update) | async-done | bytes 18874384 | tf_op jit(solution)/shard_map/all_gather | solution.py:82
  246.0 0.0 copy-done.6
  246.0 0.0 copy-done.7
  246.0 16.6 %fusion.42 = bf16[512,1536]{1,0:T(8,128)(2,1)} fusion(bf16[6144,1536]{1,0:T(8,128)(2,1)} %all-gather.6.cloned.1.call-done, bf16[512,1536]{1,0:T(8,128)(2,1)S(1)} %fusion.41, f32[1536]{0:T(1024)S(1)} %copy-done.6, f32[1536]{0:T(1024)S(1)} %copy-done.7, bf16[512,6144]{1,0:T(8,128)(2,1)} %fusion.2.clone.12), kind=kOutput, calls=%fused_computation.55 | convolution fusion | flops 9667608576 | bytes 28323840 | tf_op jit(solution)/shard_map/dot_general | solution.py:81
  (9 shorter events, 0.1 us)
Async XLA Ops:
  6.5 1.5 copy-start.4
  6.5 138.8 %all-gather.4.cloned.1.call-start = ((), (), s32[]{:S(2)}) async-start(), calls=%async_computation.2 | async-start | bytes 21233664 | tf_op jit(solution)/shard_map/all_gather | solution.py:78
  7.3 68.3 %copy-start.8 = (bf16[1536]{0:T(1024)(128)(2,1)S(1)}, bf16[1536]{0:T(1024)(128)(2,1)}, u32[]{:S(2)}) copy-start(bf16[1536]{0:T(1024)(128)(2,1)} %param.14) | copy-start | bytes 9220
  7.3 238.7 %all-gather.6.cloned.1.call-start = ((), (), s32[]{:S(2)}) async-start(), calls=%async_computation.3 | async-start | bytes 21233664 | tf_op jit(solution)/shard_map/all_gather | solution.py:82
  17.7 57.9 %all-to-all-start.1 = ((bf16[8,96,1536]{2,1,0:T(8,128)(2,1)}), bf16[8,96,1536]{2,1,0:T(8,128)(2,1)}, u32[]{:S(2)}, u32[]{:S(2)}) async-start(bf16[8,96,1536]{2,1,0:T(8,128)(2,1)} %bitcast.1), calls=%async_computation.1 | async-start | bytes 4718592 | tf_op jit(solution)/shard_map/all_to_all | solution.py:51
  75.6 8.0 %copy-start.5 = (bf16[768]{0:T(1024)(128)(2,1)S(1)}, bf16[768]{0:T(1024)(128)(2,1)}, u32[]{:S(2)}) copy-start(bf16[768]{0:T(1024)(128)(2,1)} %param.20) | copy-start | bytes 4612
  78.7 17.0 %copy-start = (f32[7,7,1536]{2,1,0:T(8,128)S(1)}, f32[7,7,1536]{2,1,0:T(8,128)}, u32[]{:S(2)}) copy-start(f32[7,7,1536]{2,1,0:T(8,128)} %param.15) | copy-start | bytes 903172
  78.7 13.0 %collective-permute-start = (bf16[3,16,1536]{2,1,0:T(8,128)(2,1)S(1)}, bf16[3,16,1536]{2,1,0:T(8,128)(2,1)S(1)}, u32[]{:S(2)}, u32[]{:S(2)}) collective-permute-start(bf16[3,16,1536]{2,1,0:T(8,128)(2,1)S(1)} %bitcast.27), channel_id=1, source_target_pairs={{0,8},{8,16},{16,24},{1,9},{9,17},{17,25},{2,10},{10,18},{18,26},{... | collective-permute-start | bytes 442376 | tf_op jit(solution)/shard_map/ppermute | solution.py:18
  82.2 9.5 %collective-permute-start.1 = (bf16[3,16,1536]{2,1,0:T(8,128)(2,1)S(1)}, bf16[3,16,1536]{2,1,0:T(8,128)(2,1)S(1)}, u32[]{:S(2)}, u32[]{:S(2)}) collective-permute-start(bf16[3,16,1536]{2,1,0:T(8,128)(2,1)S(1)} %bitcast.26), channel_id=1, source_target_pairs={{8,0},{16,8},{24,16},{9,1},{17,9},{25,17},{10,2},{18,10},{26,18},{... | collective-permute-start | bytes 442376 | tf_op jit(solution)/shard_map/ppermute | solution.py:20
  92.1 4.4 %collective-permute-start.2 = (bf16[38,3,1536]{2,1,0:T(4,128)(2,1)S(1)}, bf16[38,3,1536]{2,1,0:T(4,128)(2,1)S(1)}, u32[]{:S(2)}, u32[]{:S(2)}) collective-permute-start(bf16[38,3,1536]{2,1,0:T(4,128)(2,1)S(1)} %get-tuple-element.58), channel_id=1, source_target_pairs={{0,1},{1,2},{2,3},{3,4},{4,5},{5,6},{6,7},{8,9},{9,10},{10,11},{11... | collective-permute-start | bytes 1050632 | tf_op jit(solution)/shard_map/ppermute | solution.py:18
  94.4 4.5 %collective-permute-start.3 = (bf16[38,3,1536]{2,1,0:T(4,128)(2,1)S(1)}, bf16[38,3,1536]{2,1,0:T(4,128)(2,1)S(1)}, u32[]{:S(2)}, u32[]{:S(2)}) collective-permute-start(bf16[38,3,1536]{2,1,0:T(4,128)(2,1)S(1)} %get-tuple-element.59), channel_id=1, source_target_pairs={{1,0},{2,1},{3,2},{4,3},{5,4},{6,5},{7,6},{9,8},{10,9},{11,10},{12... | collective-permute-start | bytes 1050632 | tf_op jit(solution)/shard_map/ppermute | solution.py:20
  96.5 3.9 %copy-start.1 = (f32[1536]{0:T(1024)S(1)}, f32[1536]{0:T(1024)}, u32[]{:S(2)}) copy-start(f32[1536]{0:T(1024)} %param.16) | copy-start | bytes 18436
  126.7 0.7 copy-start.2
  126.7 0.7 copy-start.3
  145.3 100.7 %copy-start.6 = (f32[1536]{0:T(1024)S(1)}, f32[1536]{0:T(1024)}, u32[]{:S(2)}) copy-start(f32[1536]{0:T(1024)} %param.22) | copy-start | bytes 18436
  145.3 100.7 %copy-start.7 = (f32[1536]{0:T(1024)S(1)}, f32[1536]{0:T(1024)}, u32[]{:S(2)}) copy-start(f32[1536]{0:T(1024)} %param.23) | copy-start | bytes 18436
Sparse Core Ops, SparseCore 0:
  9.2 136.0 all-gather.3
  147.2 98.7 all-gather.5
where the time goes:
time: 270 us; the launch traced here: 269 us
  waiting for transfers between devices  134 us (50%)
  matrix products  58.7 us (22%)
  other arithmetic  30.2 us (11%)
  blocking collectives  17.8 us (7%)
  between operations  13.6 us (5%)
  starting transfers between devices  12.9 us (5%)
    all_gather x1, waiting for transfers between devices, local(): lax.all_gather(w_out, 'col', axis=0, tiled=True)  61.6 us
    all_to_all x1, waiting for transfers between devices, local(): lax.all_to_all(patches, 'col', split_axis=0, concat_axis=0, tiled=True)  51.9 us
    dot_general x1, matrix products, expand(): lax.dot_general(rows, weight_rows, (((1,), (1,)), ((), ())), preferred_el...  39 us
    reduce_sum x1, other arithmetic, local(): mean = jnp.mean(conv, axis=-1, keepdims=True)  26.2 us
    all_gather x1, waiting for transfers between devices, local(): lax.all_gather(w_in, 'col', axis=0, tiled=True)  17.3 us
    dot_general x1, matrix products, local(): jnp.dot(hidden, lax.all_gather(w_out, 'col', axis=0, tiled=True), preferr...  16.6 us
    all_to_all x1, blocking collectives, local(): lax.all_to_all(dest, 'col', split_axis=0, concat_axis=0, tiled=True)  9.62 us
    all_gather x1, blocking collectives, local(): lax.all_gather(b_in, 'col', axis=0, tiled=True)  8.15 us
  transfers between devices with their start and end apart: 7, of which 4 were waited for; matrix products, arithmetic and copies ran while one was open for 27% of the time, Pallas kernels for 0%

commit v1 on v0

--- a/solution.py
+++ b/solution.py
@@ -31,6 +31,12 @@
     return jax.nn.gelu(pre + bias_rows.astype(jnp.float32), approximate=False).astype(jnp.bfloat16)
 
 
+def mlp(rows, weight_in, bias, weight_out):
+    return jnp.dot(
+        expand(rows, weight_in, bias), weight_out, preferred_element_type=jnp.float32
+    )
+
+
 def local(
     patches,
     dest,
@@ -47,6 +53,11 @@
 ):
     cells = TH * TW
     channels = patches.shape[1]
+    count = lax.axis_size("col")
+    lines = count // 4
+    mates = [(i, i ^ 1) for i in range(count)]
+    sides = [(i, i ^ 2) for i in range(count)]
+    second = tuple(lax.ppermute(part, "col", sides) for part in (w_in, b_in, w_out))
     moved, moved_dest = (
         lax.all_to_all(patches, "col", split_axis=0, concat_axis=0, tiled=True),
         lax.all_to_all(dest, "col", split_axis=0, concat_axis=0, tiled=True),
@@ -73,14 +84,31 @@
     var = jnp.mean(centred * centred, axis=-1, keepdims=True)
     normed = (centred * lax.rsqrt(var + 1e-06) * norm_gain + norm_bias).astype(jnp.bfloat16)
     flat = normed.reshape(cells, channels)
-    hidden = expand(
-        flat,
-        lax.all_gather(w_in, "col", axis=0, tiled=True),
-        lax.all_gather(b_in, "col", axis=0, tiled=True),
-    )
-    mixed = jnp.dot(
-        hidden, lax.all_gather(w_out, "col", axis=0, tiled=True), preferred_element_type=jnp.float32
-    )
+    home, mate = flat, lax.ppermute(flat, "col", mates)
+    away = []
+    for step in range(1, lines):
+        there = lax.ppermute(flat, "col", [(i, (i + 4 * step) % count) for i in range(count)])
+        away.append((there, lax.ppermute(there, "col", mates)))
+    first = (w_in, b_in, w_out)
+    near, far = [mlp(home, *first), mlp(mate, *first)], []
+    for there, cross in away:
+        far.append([mlp(cross, *first), mlp(there, *first)])
+    back = []
+    for step, (there, cross) in enumerate(away, 1):
+        lent = (far[step - 1][0] + mlp(cross, *second)).astype(jnp.bfloat16)
+        lent = lax.ppermute(lent, "col", mates)
+        total = far[step - 1][1] + mlp(there, *second) + lent.astype(jnp.float32)
+        back.append(
+            lax.ppermute(
+                total.astype(jnp.bfloat16),
+                "col",
+                [((i + 4 * step) % count, i) for i in range(count)],
+            )
+        )
+    lent = lax.ppermute((near[1] + mlp(mate, *second)).astype(jnp.bfloat16), "col", mates)
+    mixed = near[0] + mlp(home, *second) + lent.astype(jnp.float32)
+    for part in back:
+        mixed = mixed + part.astype(jnp.float32)
     result = grid.astype(jnp.float32) + layer_scale * (mixed + b_out)
     return result.astype(jnp.bfloat16).reshape(TH, TW, channels)
 

time: 270 us -> 342 us (1.27); the launches traced: 269 us -> 337 us
  waiting for transfers between devices: 134 us -> 173 us
  matrix products: 58.7 us -> 92.7 us
  starting transfers between devices: 12.9 us -> 28.1 us
  between operations: 13.6 us -> 0.65 us
  blocking collectives: 17.8 us -> 9.62 us
    ppermute x0 -> x9, waiting for transfers between devices: none -> 140 us  [the longest x3 80.3 us: local(): lax.ppermute(part, 'col', sides)]
    all_gather x2 -> x0, waiting for transfers between devices: 78.9 us -> none  [the longest x1 61.6 us: local(): lax.all_gather(w_out, 'col', axis=0, tiled=True)]
    dot_general x2 -> x8, matrix products: 55.6 us -> 89.7 us  [mlp(): jnp.dot(expand(rows, weight_in, bias), weight_out, preferred_element_type...]
    all_to_all x1, waiting for transfers between devices: 51.9 us -> 28 us  [local(): lax.all_to_all(patches, 'col', split_axis=0, concat_axis=0, tiled=True)]
    ppermute x0 -> x9, starting transfers between devices: none -> 15 us  [the longest x1 7.56 us: local(): lax.ppermute(flat, 'col', [(i, (i + 4 * step) % count) for i in range(cou...]
    all_gather x1 -> x0, blocking collectives: 8.15 us -> none  [local(): lax.all_gather(b_in, 'col', axis=0, tiled=True)]
  transfers between devices with their start and end apart: 7 -> 14, of which waited for: 4 -> 8; matrix products, arithmetic and copies ran while one was open for 27% -> 20% of each run, Pallas kernels for 0% -> 0%
where the time goes in v1:
time: 342 us; the launch traced here: 337 us
  waiting for transfers between devices  173 us (51%)
  matrix products  92.7 us (27%)
  other arithmetic  30.6 us (9%)
  starting transfers between devices  28.1 us (8%)
  blocking collectives  9.62 us (3%)
    dot_general x8, matrix products, mlp(): jnp.dot(expand(rows, weight_in, bias), weight_out, preferred_element_type...  89.7 us
    ppermute x3, waiting for transfers between devices, local(): lax.ppermute(part, 'col', sides)  80.3 us
    ppermute x1, waiting for transfers between devices, local(): lax.ppermute(flat, 'col', [(i, (i + 4 * step) % count) for i in range(cou...  33.4 us
    all_to_all x1, waiting for transfers between devices, local(): lax.all_to_all(patches, 'col', split_axis=0, concat_axis=0, tiled=True)  28 us
    reduce_sum x1, other arithmetic, local(): mean = jnp.mean(conv, axis=-1, keepdims=True)  26.7 us
    ppermute x1, waiting for transfers between devices, local(): lax.ppermute(total.astype(jnp.bfloat16), 'col', [((i + 4 * step) % count,...  26 us
    all_to_all x1, blocking collectives, local(): lax.all_to_all(dest, 'col', split_axis=0, concat_axis=0, tiled=True)  9.62 us
    ppermute x1, starting transfers between devices, local(): lax.ppermute(flat, 'col', [(i, (i + 4 * step) % count) for i in range(cou...  7.56 us
  transfers between devices with their start and end apart: 14, of which 8 were waited for; matrix products, arithmetic and copies ran while one was open for 20% of the time, Pallas kernels for 0%

profile of v1, /device:TPU:0, one launch (start us, length us, event | category | flops | bytes accessed | tf_op | source)
XLA Modules:
  0.0 337.0 jit_solution(13466852090726362750)
XLA Ops:
  0.0 0.8 all_to_all.14
  0.8 9.6 %all_to_all.21 = s32[8,96,1]{1,2,0:T(1,128)S(1)} all-to-all(s32[8,96,1]{1,2,0:T(1,128)S(1)} %bitcast.44), channel_id=1, replica_groups=mesh['row'=4,'col'=8] {'col'}, dimensions={0} | all-to-all | bytes 6144 | tf_op jit(solution)/shard_map/all_to_all | solution.py:63
  10.4 4.5 %all-to-all-start.1 = ((bf16[8,96,1536]{2,1,0:T(8,128)(2,1)}), bf16[8,96,1536]{2,1,0:T(8,128)(2,1)}, u32[]{:S(2)}, u32[]{:S(2)}) async-start(bf16[8,96,1536]{2,1,0:T(8,128)(2,1)} %bitcast.37), calls=%async_computation.1 | async-start | bytes 4718592 | tf_op jit(solution)/shard_map/all_to_all | solution.py:62
  14.9 0.5 broadcast.1164
  15.4 0.7 reduce.101
  16.1 0.1 eq.15
  16.1 0.3 fusion.87
  16.4 28.0 %all-to-all-done.1 = bf16[8,96,1536]{2,1,0:T(8,128)(2,1)} async-done(((bf16[8,96,1536]{2,1,0:T(8,128)(2,1)}), bf16[8,96,1536]{2,1,0:T(8,128)(2,1)}, u32[]{:S(2)}, u32[]{:S(2)}) %all-to-all-start.1) | async-done | bytes 2359328 | tf_op jit(solution)/shard_map/all_to_all | solution.py:62
  44.4 3.0 fusion.10
  47.4 0.0 copy-start
  47.4 1.4 collective-permute-start.1
  48.9 4.6 %collective-permute-start = (bf16[3,16,1536]{2,1,0:T(8,128)(2,1)S(1)}, bf16[3,16,1536]{2,1,0:T(8,128)(2,1)S(1)}, u32[]{:S(2)}, u32[]{:S(2)}) collective-permute-start(bf16[3,16,1536]{2,1,0:T(8,128)(2,1)S(1)} %bitcast.42), channel_id=1, source_target_pairs={{0,8},{8,16},{16,24},{1,9},{9,17},{17,25},{2,10},{10,18},{18,26},{... | collective-permute-start | bytes 442376 | tf_op jit(solution)/shard_map/ppermute | solution.py:18
  53.4 1.2 collective-permute-done.1
  54.6 1.5 collective-permute-done
  56.1 0.4 pad_maximum_fusion.5
  56.5 1.3 collective-permute-start.2
  57.8 1.3 collective-permute-start.3
  59.1 0.2 slice_reduce_fusion.46
  59.3 0.3 slice_reduce_fusion.48
  59.6 0.3 slice_reduce_fusion.47
  59.9 0.0 copy-start.1
  60.0 2.6 collective-permute-done.3
  62.6 1.6 maximum_maximum_fusion
  64.2 26.7 %fusion.589 = (f32[32,16]{1,0:T(8,128)S(1)}, f32[32,16,1536]{2,1,0:T(8,128)S(1)}) fusion(f32[1536]{0:T(1024)S(1)} %get-tuple-element.52, bf16[38,19,1536]{2,1,0:T(8,128)(2,1)S(1)} %get-tuple-element.57, f32[1536]{0:T(1024)S(1)} %get-tuple-element.53, f32[1536]{0:T(1024)S(1)} %get-tuple-element.6, f32[1536]{0:T(1024)S(1)} %get-tuple-element.7, ...), kind=kLoop, calls=%fused_computation.736 | loop fusion | flops 121110016 | bytes 71383040 | tf_op jit(solution)/shard_map/reduce_sum | solution.py:82
  90.9 0.0 copy-start.2
  91.0 0.4 multiply_reduce_fusion
  91.4 0.2 copy-done.2
  91.6 0.0 copy-done.3
  91.6 0.6 add_convert_fusion
  92.2 7.6 %collective-permute-start.9 = (bf16[512,1536]{1,0:T(8,128)(2,1)S(1)}, bf16[512,1536]{1,0:T(8,128)(2,1)}, u32[]{:S(2)}, u32[]{:S(2)}) collective-permute-start(bf16[512,1536]{1,0:T(8,128)(2,1)S(1)} %bitcast.38), channel_id=1, source_target_pairs={{0,4},{1,5},{2,6},{3,7},{4,0},{5,1},{6,2},{7,3},{8,12},{9,13},{10,... | collective-permute-start | bytes 4718600 | tf_op jit(solution)/shard_map/ppermute | solution.py:90
  99.8 1.1 collective-permute-start.7
  100.9 33.4 %collective-permute-done.9 = bf16[512,1536]{1,0:T(8,128)(2,1)} collective-permute-done((bf16[512,1536]{1,0:T(8,128)(2,1)S(1)}, bf16[512,1536]{1,0:T(8,128)(2,1)}, u32[]{:S(2)}, u32[]{:S(2)}) %collective-permute-start.9) | collective-permute-done | bytes 1572896 | tf_op jit(solution)/shard_map/ppermute | solution.py:90
  134.3 0.7 collective-permute-start.10
  135.0 3.1 collective-permute-start.5
  138.0 0.0 collective-permute-start.6
  138.1 2.0 collective-permute-start.4
  140.1 10.9 %fusion.98 = f32[512,1536]{1,0:T(8,128)} fusion(bf16[768,1536]{1,0:T(8,128)(2,1)} %param.21, bf16[512,1536]{1,0:T(8,128)(2,1)} %collective-permute-done.7, bf16[768,1536]{1,0:T(8,128)(2,1)} %param.19, f32[768]{0:T(1024)S(1)} %convert_element_type.270), kind=kOutput, calls=%fused_computation.191 | convolution fusion | flops 2441871360 | bytes 9440256 | tf_op jit(solution)/shard_map/dot_general | solution.py:35
  151.0 11.0 %fusion.96 = f32[512,1536]{1,0:T(8,128)} fusion(bf16[768,1536]{1,0:T(8,128)(2,1)} %param.21, bf16[512,1536]{1,0:T(8,128)(2,1)} %collective-permute-done.10, bf16[768,1536]{1,0:T(8,128)(2,1)} %param.19, f32[768]{0:T(1024)S(1)} %convert_element_type.270), kind=kOutput, calls=%fused_computation.189 | convolution fusion | flops 2441871360 | bytes 9440256 | tf_op jit(solution)/shard_map/dot_general | solution.py:35
  162.0 30.5 %collective-permute-done.6 = bf16[768,1536]{1,0:T(8,128)(2,1)} collective-permute-done((bf16[768,1536]{1,0:T(8,128)(2,1)}, bf16[768,1536]{1,0:T(8,128)(2,1)}, u32[]{:S(2)}, u32[]{:S(2)}) %collective-permute-start.6) | collective-permute-done | bytes 2359328 | tf_op jit(solution)/shard_map/ppermute | solution.py:60
  192.5 49.8 %collective-permute-done.4 = bf16[768,1536]{1,0:T(8,128)(2,1)} collective-permute-done((bf16[768,1536]{1,0:T(8,128)(2,1)}, bf16[768,1536]{1,0:T(8,128)(2,1)}, u32[]{:S(2)}, u32[]{:S(2)}) %collective-permute-start.4) | collective-permute-done | bytes 2359328 | tf_op jit(solution)/shard_map/ppermute | solution.py:60
  242.2 11.3 %fusion.9 = bf16[512,1536]{1,0:T(8,128)(2,1)} fusion(f32[512,1536]{1,0:T(8,128)} %fusion.96, bf16[768,1536]{1,0:T(8,128)(2,1)} %collective-permute-done.6, bf16[512,1536]{1,0:T(8,128)(2,1)} %collective-permute-done.10, bf16[768,1536]{1,0:T(8,128)(2,1)} %collective-permute-done.4, f32[768]{0:T(1024)S(1)} %convert_element_type.272), kind=kOutput, calls=%fused_computation.17 | convolution fusion | flops 2443444224 | bytes 11013120 | tf_op jit(solution)/shard_map/dot_general | solution.py:35
  253.5 11.3 %fusion.8 = bf16[512,1536]{1,0:T(8,128)(2,1)} fusion(f32[512,1536]{1,0:T(8,128)} %fusion.98, bf16[768,1536]{1,0:T(8,128)(2,1)} %collective-permute-done.6, bf16[512,1536]{1,0:T(8,128)(2,1)} %collective-permute-done.7, bf16[768,1536]{1,0:T(8,128)(2,1)} %collective-permute-done.4, f32[768]{0:T(1024)S(1)} %convert_element_type.272), kind=kOutput, calls=%fused_computation.16 | convolution fusion | flops 2443444224 | bytes 11013120 | tf_op jit(solution)/shard_map/dot_general | solution.py:35
  264.8 0.5 collective-permute-start.8
  265.3 11.1 %fusion.97 = f32[512,1536]{1,0:T(8,128)} fusion(bf16[768,1536]{1,0:T(8,128)(2,1)} %param.21, bf16[512,1536]{1,0:T(8,128)(2,1)} %collective-permute-done.9, bf16[768,1536]{1,0:T(8,128)(2,1)} %param.19, f32[768]{0:T(1024)S(1)} %convert_element_type.270), kind=kOutput, calls=%fused_computation.190 | convolution fusion | flops 2441871360 | bytes 9440256 | tf_op jit(solution)/shard_map/dot_general | solution.py:35
  276.4 11.7 %fusion.6 = bf16[512,1536]{1,0:T(8,128)(2,1)} fusion(bf16[512,1536]{1,0:T(8,128)(2,1)} %collective-permute-done.11, f32[512,1536]{1,0:T(8,128)} %fusion.97, bf16[768,1536]{1,0:T(8,128)(2,1)} %collective-permute-done.6, bf16[512,1536]{1,0:T(8,128)(2,1)} %collective-permute-done.9, bf16[768,1536]{1,0:T(8,128)(2,1)} %collective-permute-done.4, ...), kind=kOutput, calls=%fused_computation.14 | convolution fusion | flops 2445017088 | bytes 12585984 | tf_op jit(solution)/shard_map/dot_general | solution.py:35
  288.1 10.7 %fusion.99 = f32[512,1536]{1,0:T(8,128)} fusion(bf16[768,1536]{1,0:T(8,128)(2,1)} %param.21, bf16[512,1536]{1,0:T(8,128)(2,1)S(1)} %bitcast.40, bf16[768,1536]{1,0:T(8,128)(2,1)} %param.19, f32[768]{0:T(1024)S(1)} %convert_element_type.270), kind=kOutput, calls=%fused_computation.192 | convolution fusion | flops 2441871360 | bytes 9440256 | tf_op jit(solution)/shard_map/dot_general | solution.py:35
  298.7 26.0 %collective-permute-done.12 = bf16[512,1536]{1,0:T(8,128)(2,1)} collective-permute-done((bf16[512,1536]{1,0:T(8,128)(2,1)}, bf16[512,1536]{1,0:T(8,128)(2,1)}, u32[]{:S(2)}, u32[]{:S(2)}) %collective-permute-start.12) | collective-permute-done | bytes 1572896 | tf_op jit(solution)/shard_map/ppermute | solution.py:102
  324.7 11.8 %fusion.7 = bf16[512,1536]{1,0:T(8,128)(2,1)} fusion(bf16[512,1536]{1,0:T(8,128)(2,1)} %collective-permute-done.12, bf16[512,1536]{1,0:T(8,128)(2,1)} %collective-permute-done.8, f32[512,1536]{1,0:T(8,128)} %fusion.99, bf16[768,1536]{1,0:T(8,128)(2,1)} %collective-permute-done.6, bf16[512,1536]{1,0:T(8,128)(2,1)S(1)} %fusion.10, f32[1536]{0:T(1024)S(1)} %copy-done.5, ...), kind=kOutput, calls=%fused_computation.15 | convolution fusion | flops 2449735680 | bytes 15744000 | tf_op jit(solution)/shard_map/dot_general | solution.py:35
  (24 shorter events, 0.1 us)
Async XLA Ops:
  10.4 34.0 %copy-start.7 = (bf16[1536]{0:T(1024)(128)(2,1)S(1)}, bf16[1536]{0:T(1024)(128)(2,1)}, u32[]{:S(2)}) copy-start(bf16[1536]{0:T(1024)(128)(2,1)} %param.14) | copy-start | bytes 9220
  10.4 34.0 %all-to-all-start.1 = ((bf16[8,96,1536]{2,1,0:T(8,128)(2,1)}), bf16[8,96,1536]{2,1,0:T(8,128)(2,1)}, u32[]{:S(2)}, u32[]{:S(2)}) async-start(bf16[8,96,1536]{2,1,0:T(8,128)(2,1)} %bitcast.37), calls=%async_computation.1 | async-start | bytes 4718592 | tf_op jit(solution)/shard_map/all_to_all | solution.py:62
  47.4 11.7 %copy-start = (f32[7,7,1536]{2,1,0:T(8,128)S(1)}, f32[7,7,1536]{2,1,0:T(8,128)}, u32[]{:S(2)}) copy-start(f32[7,7,1536]{2,1,0:T(8,128)} %param.15) | copy-start | bytes 903172
  47.4 7.2 %collective-permute-start.1 = (bf16[3,16,1536]{2,1,0:T(8,128)(2,1)S(1)}, bf16[3,16,1536]{2,1,0:T(8,128)(2,1)S(1)}, u32[]{:S(2)}, u32[]{:S(2)}) collective-permute-start(bf16[3,16,1536]{2,1,0:T(8,128)(2,1)S(1)} %bitcast.43), channel_id=1, source_target_pairs={{8,0},{16,8},{24,16},{9,1},{17,9},{25,17},{10,2},{18,10},{26,18},{... | collective-permute-start | bytes 442376 | tf_op jit(solution)/shard_map/ppermute | solution.py:20
  48.9 7.2 %collective-permute-start = (bf16[3,16,1536]{2,1,0:T(8,128)(2,1)S(1)}, bf16[3,16,1536]{2,1,0:T(8,128)(2,1)S(1)}, u32[]{:S(2)}, u32[]{:S(2)}) collective-permute-start(bf16[3,16,1536]{2,1,0:T(8,128)(2,1)S(1)} %bitcast.42), channel_id=1, source_target_pairs={{0,8},{8,16},{16,24},{1,9},{9,17},{17,25},{2,10},{10,18},{18,26},{... | collective-permute-start | bytes 442376 | tf_op jit(solution)/shard_map/ppermute | solution.py:18
  56.5 3.5 %collective-permute-start.2 = (bf16[38,3,1536]{2,1,0:T(4,128)(2,1)S(1)}, bf16[38,3,1536]{2,1,0:T(4,128)(2,1)S(1)}, u32[]{:S(2)}, u32[]{:S(2)}) collective-permute-start(bf16[38,3,1536]{2,1,0:T(4,128)(2,1)S(1)} %get-tuple-element.58), channel_id=1, source_target_pairs={{0,1},{1,2},{2,3},{3,4},{4,5},{5,6},{6,7},{8,9},{9,10},{10,11},{11... | collective-permute-start | bytes 1050632 | tf_op jit(solution)/shard_map/ppermute | solution.py:18
  57.8 4.8 %collective-permute-start.3 = (bf16[38,3,1536]{2,1,0:T(4,128)(2,1)S(1)}, bf16[38,3,1536]{2,1,0:T(4,128)(2,1)S(1)}, u32[]{:S(2)}, u32[]{:S(2)}) collective-permute-start(bf16[38,3,1536]{2,1,0:T(4,128)(2,1)S(1)} %get-tuple-element.59), channel_id=1, source_target_pairs={{1,0},{2,1},{3,2},{4,3},{5,4},{6,5},{7,6},{9,8},{10,9},{11,10},{12... | collective-permute-start | bytes 1050632 | tf_op jit(solution)/shard_map/ppermute | solution.py:20
  59.9 4.3 %copy-start.1 = (f32[1536]{0:T(1024)S(1)}, f32[1536]{0:T(1024)}, u32[]{:S(2)}) copy-start(f32[1536]{0:T(1024)} %param.16) | copy-start | bytes 18436
  90.9 0.7 copy-start.2
  90.9 0.7 copy-start.3
  91.6 43.3 %copy-start.4 = (bf16[768]{0:T(1024)(128)(2,1)S(1)}, bf16[768]{0:T(1024)(128)(2,1)}, u32[]{:S(2)}) copy-start(bf16[768]{0:T(1024)(128)(2,1)} %param.20) | copy-start | bytes 4612
  92.2 42.1 %collective-permute-start.9 = (bf16[512,1536]{1,0:T(8,128)(2,1)S(1)}, bf16[512,1536]{1,0:T(8,128)(2,1)}, u32[]{:S(2)}, u32[]{:S(2)}) collective-permute-start(bf16[512,1536]{1,0:T(8,128)(2,1)S(1)} %bitcast.38), channel_id=1, source_target_pairs={{0,4},{1,5},{2,6},{3,7},{4,0},{5,1},{6,2},{7,3},{8,12},{9,13},{10,... | collective-permute-start | bytes 4718600 | tf_op jit(solution)/shard_map/ppermute | solution.py:90
  99.8 40.3 %collective-permute-start.7 = (bf16[512,1536]{1,0:T(8,128)(2,1)S(1)}, bf16[512,1536]{1,0:T(8,128)(2,1)}, u32[]{:S(2)}, u32[]{:S(2)}) collective-permute-start(bf16[512,1536]{1,0:T(8,128)(2,1)S(1)} %bitcast.39), channel_id=1, source_target_pairs={{0,1},{1,0},{2,3},{3,2},{4,5},{5,4},{6,7},{7,6},{8,9},{9,8},{10,11... | collective-permute-start | bytes 4718600 | tf_op jit(solution)/shard_map/ppermute | solution.py:87
  134.3 16.7 %collective-permute-start.10 = (bf16[512,1536]{1,0:T(8,128)(2,1)}, bf16[512,1536]{1,0:T(8,128)(2,1)}, u32[]{:S(2)}, u32[]{:S(2)}) collective-permute-start(bf16[512,1536]{1,0:T(8,128)(2,1)} %collective-permute-done.9), channel_id=1, source_target_pairs={{0,1},{1,0},{2,3},{3,2},{4,5},{5,4},{6,7},{7,6},{8,9},{9,8},{10,11... | collective-permute-start | bytes 4718600 | tf_op jit(solution)/shard_map/ppermute | solution.py:91
  135.0 5.1 %collective-permute-start.5 = (bf16[768]{0:T(1024)(128)(2,1)S(1)}, bf16[768]{0:T(1024)(128)(2,1)S(1)}, u32[]{:S(2)}, u32[]{:S(2)}) collective-permute-start(bf16[768]{0:T(1024)(128)(2,1)S(1)} %copy-done.4), channel_id=1, source_target_pairs={{0,2},{1,3},{2,0},{3,1},{4,6},{5,7},{6,4},{7,5},{8,10},{9,11},{10,... | collective-permute-start | bytes 4616 | tf_op jit(solution)/shard_map/ppermute | solution.py:60
  138.0 54.4 %collective-permute-start.6 = (bf16[768,1536]{1,0:T(8,128)(2,1)}, bf16[768,1536]{1,0:T(8,128)(2,1)}, u32[]{:S(2)}, u32[]{:S(2)}) collective-permute-start(bf16[768,1536]{1,0:T(8,128)(2,1)} %param.21), channel_id=1, source_target_pairs={{0,2},{1,3},{2,0},{3,1},{4,6},{5,7},{6,4},{7,5},{8,10},{9,11},{10,... | collective-permute-start | bytes 7077896 | tf_op jit(solution)/shard_map/ppermute | solution.py:60
  138.1 104.2 %collective-permute-start.4 = (bf16[768,1536]{1,0:T(8,128)(2,1)}, bf16[768,1536]{1,0:T(8,128)(2,1)}, u32[]{:S(2)}, u32[]{:S(2)}) collective-permute-start(bf16[768,1536]{1,0:T(8,128)(2,1)} %param.19), channel_id=1, source_target_pairs={{0,2},{1,3},{2,0},{3,1},{4,6},{5,7},{6,4},{7,5},{8,10},{9,11},{10,... | collective-permute-start | bytes 7077896 | tf_op jit(solution)/shard_map/ppermute | solution.py:60
  253.5 22.8 %collective-permute-start.11 = (bf16[512,1536]{1,0:T(8,128)(2,1)}, bf16[512,1536]{1,0:T(8,128)(2,1)}, u32[]{:S(2)}, u32[]{:S(2)}) collective-permute-start(bf16[512,1536]{1,0:T(8,128)(2,1)} %fusion.9), channel_id=1, source_target_pairs={{0,1},{1,0},{2,3},{3,2},{4,5},{5,4},{6,7},{7,6},{8,9},{9,8},{10,11... | collective-permute-start | bytes 4718600 | tf_op jit(solution)/shard_map/ppermute | solution.py:99
  264.8 34.0 %collective-permute-start.8 = (bf16[512,1536]{1,0:T(8,128)(2,1)}, bf16[512,1536]{1,0:T(8,128)(2,1)}, u32[]{:S(2)}, u32[]{:S(2)}) collective-permute-start(bf16[512,1536]{1,0:T(8,128)(2,1)} %fusion.8), channel_id=1, source_target_pairs={{0,1},{1,0},{2,3},{3,2},{4,5},{5,4},{6,7},{7,6},{8,9},{9,8},{10,11... | collective-permute-start | bytes 4718600 | tf_op jit(solution)/shard_map/ppermute | solution.py:108
  288.1 36.6 %copy-start.5 = (f32[1536]{0:T(1024)S(1)}, f32[1536]{0:T(1024)}, u32[]{:S(2)}) copy-start(f32[1536]{0:T(1024)} %param.22) | copy-start | bytes 18436
  288.1 36.6 %copy-start.6 = (f32[1536]{0:T(1024)S(1)}, f32[1536]{0:T(1024)}, u32[]{:S(2)}) copy-start(f32[1536]{0:T(1024)} %param.23) | copy-start | bytes 18436
  288.1 36.6 %collective-permute-start.12 = (bf16[512,1536]{1,0:T(8,128)(2,1)}, bf16[512,1536]{1,0:T(8,128)(2,1)}, u32[]{:S(2)}, u32[]{:S(2)}) collective-permute-start(bf16[512,1536]{1,0:T(8,128)(2,1)} %fusion.6), channel_id=1, source_target_pairs={{4,0},{5,1},{6,2},{7,3},{0,4},{1,5},{2,6},{3,7},{12,8},{13,9},{14,... | collective-permute-start | bytes 4718600 | tf_op jit(solution)/shard_map/ppermute | solution.py:102

commit v2 on v0

--- a/solution.py
+++ b/solution.py
@@ -47,6 +47,20 @@
 ):
     cells = TH * TW
     channels = patches.shape[1]
+    count = lax.axis_size("col")
+    chips = count // 2
+    mates = [(i, i ^ 1) for i in range(count)]
+    groups = [[2 * chip + core for chip in range(chips)] for core in range(2)]
+    some_in, some_out = (
+        lax.all_gather(part, "col", axis=0, tiled=True, axis_index_groups=groups)
+        for part in (w_in, w_out)
+    )
+    shifted = [b_in] + [
+        lax.ppermute(b_in, "col", [(i, (i + 2 * step) % count) for i in range(count)])
+        for step in range(1, chips)
+    ]
+    order = jnp.remainder(lax.axis_index("col") // 2 - jnp.arange(chips), chips)
+    some_bias = jnp.take(jnp.stack(shifted), order, axis=0).reshape(-1)
     moved, moved_dest = (
         lax.all_to_all(patches, "col", split_axis=0, concat_axis=0, tiled=True),
         lax.all_to_all(dest, "col", split_axis=0, concat_axis=0, tiled=True),
@@ -73,14 +87,13 @@
     var = jnp.mean(centred * centred, axis=-1, keepdims=True)
     normed = (centred * lax.rsqrt(var + 1e-06) * norm_gain + norm_bias).astype(jnp.bfloat16)
     flat = normed.reshape(cells, channels)
-    hidden = expand(
-        flat,
-        lax.all_gather(w_in, "col", axis=0, tiled=True),
-        lax.all_gather(b_in, "col", axis=0, tiled=True),
-    )
-    mixed = jnp.dot(
-        hidden, lax.all_gather(w_out, "col", axis=0, tiled=True), preferred_element_type=jnp.float32
-    )
+    mate = lax.ppermute(flat, "col", mates)
+    home_hidden = lax.optimization_barrier(expand(flat, some_in, some_bias))
+    mate_hidden = lax.optimization_barrier(expand(mate, some_in, some_bias))
+    lent = jnp.dot(mate_hidden, some_out, preferred_element_type=jnp.float32).astype(jnp.bfloat16)
+    lent = lax.ppermute(lent, "col", mates)
+    mixed = jnp.dot(home_hidden, some_out, preferred_element_type=jnp.float32)
+    mixed = mixed + lent.astype(jnp.float32)
     result = grid.astype(jnp.float32) + layer_scale * (mixed + b_out)
     return result.astype(jnp.bfloat16).reshape(TH, TW, channels)
 

time: 270 us -> 284 us (1.052)
  starting transfers between devices: 12.9 us -> 36.2 us
  blocking collectives: 17.8 us -> 9.62 us
  waiting for transfers between devices: 134 us -> 129 us
    ppermute x0 -> x5, starting transfers between devices: none -> 24.9 us  [the longest x1 21.3 us: local(): mate = lax.ppermute(flat, 'col', mates)]
    all_gather x2, waiting for transfers between devices: 78.9 us -> 66.9 us  [local(): lax.all_gather(part, 'col', axis=0, tiled=True, axis_index_groups=groups)]
    all_gather x1 -> x0, blocking collectives: 8.15 us -> none  [local(): lax.all_gather(b_in, 'col', axis=0, tiled=True)]
    ppermute x2, waiting for transfers between devices: 2.29 us -> 5.94 us  [extended(): lax.ppermute(head, axis, [((i + 1) % count, i) for i in range(ends)])]
    dot_general x1 -> x2, matrix products: 39 us -> 41 us  [expand(): lax.dot_general(rows, weight_rows, (((1,), (1,)), ((), ())), preferred_el...]
    dot_general x1 -> x2, matrix products: 16.6 us -> 15.9 us  [the longest x1 9.52 us: local(): jnp.dot(mate_hidden, some_out, preferred_element_type=jnp.float32)]
  transfers between devices with their start and end apart: 7 -> 12, of which waited for: 4 -> 7; matrix products, arithmetic and copies ran while one was open for 27% -> 27% of each run, Pallas kernels for 0% -> 0%
where the time goes in v2:
time: 284 us
  waiting for transfers between devices  129 us (45%)
  matrix products  59.9 us (21%)
  starting transfers between devices  36.2 us (13%)
  other arithmetic  30.3 us (11%)
  between operations  13.8 us (5%)
  blocking collectives  9.62 us (3%)
  local copies, waits for them, and re-layouts  4.47 us (2%)
    all_gather x2, waiting for transfers between devices, local(): lax.all_gather(part, 'col', axis=0, tiled=True, axis_index_groups=groups)  66.9 us
    all_to_all x1, waiting for transfers between devices, local(): lax.all_to_all(patches, 'col', split_axis=0, concat_axis=0, tiled=True)  51.7 us
    dot_general x2, matrix products, expand(): lax.dot_general(rows, weight_rows, (((1,), (1,)), ((), ())), preferred_el...  41 us
    reduce_sum x1, other arithmetic, local(): mean = jnp.mean(conv, axis=-1, keepdims=True)  26.2 us
    ppermute x1, starting transfers between devices, local(): mate = lax.ppermute(flat, 'col', mates)  21.3 us
    all_to_all x1, blocking collectives, local(): lax.all_to_all(dest, 'col', split_axis=0, concat_axis=0, tiled=True)  9.62 us
    dot_general x1, matrix products, local(): jnp.dot(mate_hidden, some_out, preferred_element_type=jnp.float32)  9.52 us
    dot_general x1, matrix products, local(): mixed = jnp.dot(home_hidden, some_out, preferred_element_type=jnp.float32)  6.33 us
  transfers between devices with their start and end apart: 12, of which 7 were waited for; matrix products, arithmetic and copies ran while one was open for 27% of the time, Pallas kernels for 0%

profile of v2, /device:TPU:0, one launch (start us, length us, event | category | flops | bytes accessed | tf_op | source)
XLA Modules:
  0.0 283.6 jit_solution(15459676722648844880)
XLA Ops:
  6.5 0.7 all-gather.3.cloned.1.call-update
  7.3 0.8 all_to_all.14
  8.0 9.6 %all_to_all.21 = s32[8,96,1]{1,2,0:T(1,128)S(1)} all-to-all(s32[8,96,1]{1,2,0:T(1,128)S(1)} %bitcast.29), channel_id=1, replica_groups=mesh['row'=4,'col'=8] {'col'}, dimensions={0} | all-to-all | bytes 6144 | tf_op jit(solution)/shard_map/all_to_all | solution.py:66
  17.6 3.8 %all-to-all-start.1 = ((bf16[8,96,1536]{2,1,0:T(8,128)(2,1)}), bf16[8,96,1536]{2,1,0:T(8,128)(2,1)S(1)}, u32[]{:S(2)}, u32[]{:S(2)}) async-start(bf16[8,96,1536]{2,1,0:T(8,128)(2,1)} %bitcast.23), calls=%async_computation.1 | async-start | bytes 4718592 | tf_op jit(solution)/shard_map/all_to_all | solution.py:65
  21.5 0.0 all-gather.5.cloned.1.call-start
  21.5 0.7 all-gather.5.cloned.1.call-update
  22.2 0.5 broadcast.372
  22.7 0.7 reduce.101
  23.4 0.1 eq.17
  23.5 0.3 fusion.25
  23.7 51.7 %all-to-all-done.1 = bf16[8,96,1536]{2,1,0:T(8,128)(2,1)S(1)} async-done(((bf16[8,96,1536]{2,1,0:T(8,128)(2,1)}), bf16[8,96,1536]{2,1,0:T(8,128)(2,1)S(1)}, u32[]{:S(2)}, u32[]{:S(2)}) %all-to-all-start.1) | async-done | bytes 2359328 | tf_op jit(solution)/shard_map/all_to_all | solution.py:65
  75.4 1.4 copy-done
  76.8 3.0 %fusion.20 = bf16[512,1536]{1,0:T(8,128)(2,1)S(1)} fusion(bf16[768,1536]{1,0:T(8,128)(2,1)} %bitcast.24, bf16[1536]{0:T(1024)(128)(2,1)S(1)} %copy-done.9, pred[512]{0:T(512)(128)(4,1)S(1)} %fusion.25, s32[768]{0:T(1024)S(1)} %eq.17), kind=kOutput, calls=%fused_computation.44 | convolution fusion | flops 1209139200 | bytes 3938816 | tf_op jit(solution)/shard_map/dot_general | solution.py:70
  79.9 0.0 copy-start.1
  79.9 3.5 %collective-permute-start = (bf16[3,16,1536]{2,1,0:T(8,128)(2,1)S(1)}, bf16[3,16,1536]{2,1,0:T(8,128)(2,1)S(1)}, u32[]{:S(2)}, u32[]{:S(2)}) collective-permute-start(bf16[3,16,1536]{2,1,0:T(8,128)(2,1)S(1)} %bitcast.28), channel_id=1, source_target_pairs={{0,8},{8,16},{16,24},{1,9},{9,17},{17,25},{2,10},{10,18},{18,26},{... | collective-permute-start | bytes 442376 | tf_op jit(solution)/shard_map/ppermute | solution.py:18
  83.5 1.3 collective-permute-start.1
  84.8 1.3 collective-permute-done
  86.1 4.4 %collective-permute-done.1 = bf16[3,16,1536]{2,1,0:T(8,128)(2,1)S(1)} collective-permute-done((bf16[3,16,1536]{2,1,0:T(8,128)(2,1)S(1)}, bf16[3,16,1536]{2,1,0:T(8,128)(2,1)S(1)}, u32[]{:S(2)}, u32[]{:S(2)}) %collective-permute-start.1) | collective-permute-done | bytes 147488 | tf_op jit(solution)/shard_map/ppermute | solution.py:20
  90.5 0.4 pad_maximum_fusion.5
  90.9 1.3 collective-permute-start.2
  92.2 1.3 collective-permute-start.3
  93.5 0.2 slice_reduce_fusion.46
  93.7 0.3 slice_reduce_fusion.48
  94.0 0.3 slice_reduce_fusion.47
  94.4 1.5 collective-permute-done.3
  95.9 1.6 maximum_maximum_fusion
  97.6 26.2 %fusion.30 = (f32[32,16]{1,0:T(8,128)S(1)}, f32[32,16,1536]{2,1,0:T(8,128)S(1)}) fusion(f32[1536]{0:T(1024)S(1)} %get-tuple-element.52, bf16[38,19,1536]{2,1,0:T(8,128)(2,1)S(1)} %get-tuple-element.57, f32[1536]{0:T(1024)S(1)} %get-tuple-element.53, f32[1536]{0:T(1024)S(1)} %get-tuple-element.6, f32[1536]{0:T(1024)S(1)} %get-tuple-element.7, ...), kind=kLoop, calls=%fused_computation.134 | loop fusion | flops 121110016 | bytes 71383040 | tf_op jit(solution)/shard_map/reduce_sum | solution.py:85
  123.8 0.0 copy-start.4
  123.8 0.4 multiply_reduce_fusion
  124.2 0.0 copy-start.5
  124.3 0.2 copy-done.3
  124.5 0.0 copy-done.4
  124.5 0.6 add_convert_fusion.1
  125.1 21.3 %collective-permute-start.7 = (bf16[512,1536]{1,0:T(8,128)(2,1)S(1)}, bf16[512,1536]{1,0:T(8,128)(2,1)}, u32[]{:S(2)}, u32[]{:S(2)}) collective-permute-start(bf16[512,1536]{1,0:T(8,128)(2,1)S(1)} %bitcast.25), channel_id=1, source_target_pairs={{0,1},{1,0},{2,3},{3,2},{4,5},{5,4},{6,7},{7,6},{8,9},{9,8},{10,11... | collective-permute-start | bytes 4718600 | tf_op jit(solution)/shard_map/ppermute | solution.py:90
  146.4 2.0 collective-permute-start.4
  148.4 1.5 collective-permute-start.6
  149.9 0.9 collective-permute-done.4
  150.9 1.1 collective-permute-done.5
  152.1 0.6 gather_fusion
  152.6 0.1 select_convert_fusion
  152.7 0.0 all-gather.3.cloned.1.call-done
  152.8 22.1 %fusion.5 = bf16[512,3072]{1,0:T(8,128)(2,1)} fusion(bf16[512,1536]{1,0:T(8,128)(2,1)} %collective-permute-done.7, bf16[3072,1536]{1,0:T(8,128)(2,1)} %all-gather.3.cloned.1.call-done, f32[3072]{0:T(1024)S(1)} %reshape.110), kind=kOutput, calls=%fused_computation.8 | convolution fusion | flops 4935647232 | bytes 14168064 | tf_op jit(solution)/shard_map/dot_general | solution.py:28
  174.9 66.9 %all-gather.5.cloned.1.call-done = bf16[3072,1536]{1,0:T(8,128)(2,1)} async-done(((bf16[768,1536]{1,0:T(8,128)(2,1)}), bf16[3072,1536]{1,0:T(8,128)(2,1)}) %all-gather.5.cloned.1.call-update) | async-done | bytes 9437200 | tf_op jit(solution)/shard_map/all_gather | solution.py:55
  241.8 9.5 %convolution_convert_fusion = bf16[512,1536]{1,0:T(8,128)(2,1)S(1)} fusion(bf16[512,3072]{1,0:T(8,128)(2,1)} %fusion.5, bf16[3072,1536]{1,0:T(8,128)(2,1)} %all-gather.5.cloned.1.call-done), kind=kOutput, calls=%fused_computation.45 | convolution fusion | flops 4832624640 | bytes 14155776 | tf_op jit(solution)/shard_map/dot_general | solution.py:93
  251.3 0.0 copy-start.8
  251.3 0.1 collective-permute-start.8
  251.4 18.9 %fusion.2 = bf16[512,3072]{1,0:T(8,128)(2,1)S(1)} fusion(bf16[512,1536]{1,0:T(8,128)(2,1)S(1)} %bitcast.26, bf16[3072,1536]{1,0:T(8,128)(2,1)S(1)} %copy-done.6, f32[3072]{0:T(1024)S(1)} %reshape.110), kind=kOutput, calls=%fused_computation.5 | convolution fusion | flops 4935647232 | bytes 14168064 | tf_op jit(solution)/shard_map/dot_general | solution.py:28
  270.4 6.3 %add_convert_fusion = bf16[512,1536]{1,0:T(8,128)(2,1)} fusion(bf16[512,1536]{1,0:T(8,128)(2,1)S(1)} %collective-permute-done.8, bf16[512,1536]{1,0:T(8,128)(2,1)S(1)} %fusion.20, f32[1536]{0:T(1024)S(1)} %copy-done.7, f32[1536]{0:T(1024)S(1)} %copy-done.8, bf16[512,3072]{1,0:T(8,128)(2,1)S(1)} %fusion.2, bf16[3072,1536]{1,0:T(8,128)(2,1)S(1)} %bitcast.31), kind=kOutput, calls=%fused_computation.40 | convolution fusion | flops 4837343232 | bytes 17313792 | tf_op jit(solution)/shard_map/dot_general | solution.py:95
  (38 shorter events, 0.2 us)
Async XLA Ops:
  6.5 146.2 %all-gather.3.cloned.1.call-start = ((), (), s32[]{:S(2)}) async-start(), calls=%async_computation.2 | async-start | bytes 11796480 | tf_op jit(solution)/shard_map/all_gather | solution.py:55
  17.6 59.2 %copy-start.9 = (bf16[1536]{0:T(1024)(128)(2,1)S(1)}, bf16[1536]{0:T(1024)(128)(2,1)}, u32[]{:S(2)}) copy-start(bf16[1536]{0:T(1024)(128)(2,1)} %param.14) | copy-start | bytes 9220
  17.6 57.8 %all-to-all-start.1 = ((bf16[8,96,1536]{2,1,0:T(8,128)(2,1)}), bf16[8,96,1536]{2,1,0:T(8,128)(2,1)S(1)}, u32[]{:S(2)}, u32[]{:S(2)}) async-start(bf16[8,96,1536]{2,1,0:T(8,128)(2,1)} %bitcast.23), calls=%async_computation.1 | async-start | bytes 4718592 | tf_op jit(solution)/shard_map/all_to_all | solution.py:65
  21.5 220.3 %all-gather.5.cloned.1.call-start = ((), (), s32[]{:S(2)}) async-start(), calls=%async_computation.3 | async-start | bytes 11796480 | tf_op jit(solution)/shard_map/all_gather | solution.py:55
  75.4 1.4 copy-start
  79.9 13.6 %copy-start.1 = (f32[7,7,1536]{2,1,0:T(8,128)S(1)}, f32[7,7,1536]{2,1,0:T(8,128)}, u32[]{:S(2)}) copy-start(f32[7,7,1536]{2,1,0:T(8,128)} %param.15) | copy-start | bytes 903172
  79.9 6.2 %collective-permute-start = (bf16[3,16,1536]{2,1,0:T(8,128)(2,1)S(1)}, bf16[3,16,1536]{2,1,0:T(8,128)(2,1)S(1)}, u32[]{:S(2)}, u32[]{:S(2)}) collective-permute-start(bf16[3,16,1536]{2,1,0:T(8,128)(2,1)S(1)} %bitcast.28), channel_id=1, source_target_pairs={{0,8},{8,16},{16,24},{1,9},{9,17},{17,25},{2,10},{10,18},{18,26},{... | collective-permute-start | bytes 442376 | tf_op jit(solution)/shard_map/ppermute | solution.py:18
  83.5 7.0 %collective-permute-start.1 = (bf16[3,16,1536]{2,1,0:T(8,128)(2,1)S(1)}, bf16[3,16,1536]{2,1,0:T(8,128)(2,1)S(1)}, u32[]{:S(2)}, u32[]{:S(2)}) collective-permute-start(bf16[3,16,1536]{2,1,0:T(8,128)(2,1)S(1)} %bitcast.27), channel_id=1, source_target_pairs={{8,0},{16,8},{24,16},{9,1},{17,9},{25,17},{10,2},{18,10},{26,18},{... | collective-permute-start | bytes 442376 | tf_op jit(solution)/shard_map/ppermute | solution.py:20
  90.9 3.5 %collective-permute-start.2 = (bf16[38,3,1536]{2,1,0:T(4,128)(2,1)S(1)}, bf16[38,3,1536]{2,1,0:T(4,128)(2,1)S(1)}, u32[]{:S(2)}, u32[]{:S(2)}) collective-permute-start(bf16[38,3,1536]{2,1,0:T(4,128)(2,1)S(1)} %get-tuple-element.58), channel_id=1, source_target_pairs={{0,1},{1,2},{2,3},{3,4},{4,5},{5,6},{6,7},{8,9},{9,10},{10,11},{11... | collective-permute-start | bytes 1050632 | tf_op jit(solution)/shard_map/ppermute | solution.py:18
  92.2 3.7 %collective-permute-start.3 = (bf16[38,3,1536]{2,1,0:T(4,128)(2,1)S(1)}, bf16[38,3,1536]{2,1,0:T(4,128)(2,1)S(1)}, u32[]{:S(2)}, u32[]{:S(2)}) collective-permute-start(bf16[38,3,1536]{2,1,0:T(4,128)(2,1)S(1)} %get-tuple-element.59), channel_id=1, source_target_pairs={{1,0},{2,1},{3,2},{4,3},{5,4},{6,5},{7,6},{9,8},{10,9},{11,10},{12... | collective-permute-start | bytes 1050632 | tf_op jit(solution)/shard_map/ppermute | solution.py:20
  94.3 3.2 %copy-start.2 = (f32[1536]{0:T(1024)S(1)}, f32[1536]{0:T(1024)}, u32[]{:S(2)}) copy-start(f32[1536]{0:T(1024)} %param.16) | copy-start | bytes 18436
  123.8 0.7 copy-start.3
  123.8 0.7 copy-start.4
  124.2 22.2 %copy-start.5 = (bf16[768]{0:T(1024)(128)(2,1)S(1)}, bf16[768]{0:T(1024)(128)(2,1)}, u32[]{:S(2)}) copy-start(bf16[768]{0:T(1024)(128)(2,1)} %param.20) | copy-start | bytes 4612
  125.1 27.7 %collective-permute-start.7 = (bf16[512,1536]{1,0:T(8,128)(2,1)S(1)}, bf16[512,1536]{1,0:T(8,128)(2,1)}, u32[]{:S(2)}, u32[]{:S(2)}) collective-permute-start(bf16[512,1536]{1,0:T(8,128)(2,1)S(1)} %bitcast.25), channel_id=1, source_target_pairs={{0,1},{1,0},{2,3},{3,2},{4,5},{5,4},{6,7},{7,6},{8,9},{9,8},{10,11... | collective-permute-start | bytes 4718600 | tf_op jit(solution)/shard_map/ppermute | solution.py:90
  146.4 4.5 %collective-permute-start.4 = (bf16[768]{0:T(1024)(128)(2,1)S(1)}, bf16[768]{0:T(1024)(128)(2,1)S(1)}, u32[]{:S(2)}, u32[]{:S(2)}) collective-permute-start(bf16[768]{0:T(1024)(128)(2,1)S(1)} %copy-done.5), channel_id=1, source_target_pairs={{0,2},{1,3},{2,4},{3,5},{4,6},{5,7},{6,0},{7,1},{8,10},{9,11},{10,... | collective-permute-start | bytes 4616 | tf_op jit(solution)/shard_map/ppermute | solution.py:59
  148.4 3.6 %collective-permute-start.5 = (bf16[768]{0:T(1024)(128)(2,1)S(1)}, bf16[768]{0:T(1024)(128)(2,1)S(1)}, u32[]{:S(2)}, u32[]{:S(2)}) collective-permute-start(bf16[768]{0:T(1024)(128)(2,1)S(1)} %copy-done.5), channel_id=1, source_target_pairs={{0,4},{1,5},{2,6},{3,7},{4,0},{5,1},{6,2},{7,3},{8,12},{9,13},{10,... | collective-permute-start | bytes 4616 | tf_op jit(solution)/shard_map/ppermute | solution.py:59
  148.4 3.6 %collective-permute-start.6 = (bf16[768]{0:T(1024)(128)(2,1)S(1)}, bf16[768]{0:T(1024)(128)(2,1)S(1)}, u32[]{:S(2)}, u32[]{:S(2)}) collective-permute-start(bf16[768]{0:T(1024)(128)(2,1)S(1)} %copy-done.5), channel_id=1, source_target_pairs={{0,6},{1,7},{2,0},{3,1},{4,2},{5,3},{6,4},{7,5},{8,14},{9,15},{10,... | collective-permute-start | bytes 4616 | tf_op jit(solution)/shard_map/ppermute | solution.py:59
  241.7 9.7 %copy-start.6 = (bf16[3072,1536]{1,0:T(8,128)(2,1)S(1)}, bf16[3072,1536]{1,0:T(8,128)(2,1)}, u32[]{:S(2)}) copy-start(bf16[3072,1536]{1,0:T(8,128)(2,1)} %all-gather.3.cloned.1.call-done) | copy-start | bytes 28311556
  241.7 28.6 %slice-start = ((s8[9437184]{0:T(1024)(128)(4,1)}), s8[4194304]{0:T(1024)(128)(4,1)S(1)}, s32[]{:S(2)}) async-start(s8[9437184]{0:T(1024)(128)(4,1)} %bitcast.30), calls=%async_computation.4 | async-start | bytes 8388608
  251.3 19.1 %slice-start.1 = ((s8[9437184]{0:T(1024)(128)(4,1)}), s8[4194304]{0:T(1024)(128)(4,1)S(1)}, s32[]{:S(2)}) async-start(s8[9437184]{0:T(1024)(128)(4,1)} %bitcast.30), calls=%async_computation.5 | async-start | bytes 8388608
  251.3 19.1 %slice-start.2 = ((s8[9437184]{0:T(1024)(128)(4,1)}), s8[1048576]{0:T(1024)(128)(4,1)S(1)}, s32[]{:S(2)}) async-start(s8[9437184]{0:T(1024)(128)(4,1)} %bitcast.30), calls=%async_computation.6 | async-start | bytes 2097152
  251.3 19.1 %copy-start.7 = (f32[1536]{0:T(1024)S(1)}, f32[1536]{0:T(1024)}, u32[]{:S(2)}) copy-start(f32[1536]{0:T(1024)} %param.22) | copy-start | bytes 18436
  251.3 19.1 %copy-start.8 = (f32[1536]{0:T(1024)S(1)}, f32[1536]{0:T(1024)}, u32[]{:S(2)}) copy-start(f32[1536]{0:T(1024)} %param.23) | copy-start | bytes 18436
  251.3 19.0 %collective-permute-start.8 = (bf16[512,1536]{1,0:T(8,128)(2,1)S(1)}, bf16[512,1536]{1,0:T(8,128)(2,1)S(1)}, u32[]{:S(2)}, u32[]{:S(2)}) collective-permute-start(bf16[512,1536]{1,0:T(8,128)(2,1)S(1)} %convolution_convert_fusion), channel_id=1, source_target_pairs={{0,1},{1,0},{2,3},{3,2},{4,5},{5,4},{6,7},{7,6},{8,9},{9,8},{10,11... | collective-permute-start | bytes 4718600 | tf_op jit(solution)/shard_map/ppermute | solution.py:94
Sparse Core Ops, SparseCore 0:
  9.2 134.2 all-gather.2
  145.4 96.3 all-gather.4

commit v3 on v1

--- a/solution.py
+++ b/solution.py
@@ -32,9 +32,8 @@
 
 
 def mlp(rows, weight_in, bias, weight_out):
-    return jnp.dot(
-        expand(rows, weight_in, bias), weight_out, preferred_element_type=jnp.float32
-    )
+    hidden = lax.optimization_barrier(expand(rows, weight_in, bias))
+    return jnp.dot(hidden, weight_out, preferred_element_type=jnp.float32)
 
 
 def local(
@@ -57,7 +56,15 @@
     lines = count // 4
     mates = [(i, i ^ 1) for i in range(count)]
     sides = [(i, i ^ 2) for i in range(count)]
-    second = tuple(lax.ppermute(part, "col", sides) for part in (w_in, b_in, w_out))
+    groups = [[i, i ^ 2] for i in range(count) if i % 4 < 2]
+    pair_in, pair_out = (
+        lax.all_gather(part, "col", axis=0, tiled=True, axis_index_groups=groups)
+        for part in (w_in, w_out)
+    )
+    other = lax.ppermute(b_in, "col", sides)
+    low = lax.axis_index("col") % 4 < 2
+    pair_bias = jnp.concatenate([jnp.where(low, b_in, other), jnp.where(low, other, b_in)])
+    pair = (pair_in, pair_bias, pair_out)
     moved, moved_dest = (
         lax.all_to_all(patches, "col", split_axis=0, concat_axis=0, tiled=True),
         lax.all_to_all(dest, "col", split_axis=0, concat_axis=0, tiled=True),
@@ -89,15 +96,12 @@
     for step in range(1, lines):
         there = lax.ppermute(flat, "col", [(i, (i + 4 * step) % count) for i in range(count)])
         away.append((there, lax.ppermute(there, "col", mates)))
-    first = (w_in, b_in, w_out)
-    near, far = [mlp(home, *first), mlp(mate, *first)], []
-    for there, cross in away:
-        far.append([mlp(cross, *first), mlp(there, *first)])
+    near = [mlp(home, *pair), mlp(mate, *pair)]
     back = []
     for step, (there, cross) in enumerate(away, 1):
-        lent = (far[step - 1][0] + mlp(cross, *second)).astype(jnp.bfloat16)
+        lent = mlp(cross, *pair).astype(jnp.bfloat16)
         lent = lax.ppermute(lent, "col", mates)
-        total = far[step - 1][1] + mlp(there, *second) + lent.astype(jnp.float32)
+        total = mlp(there, *pair) + lent.astype(jnp.float32)
         back.append(
             lax.ppermute(
                 total.astype(jnp.bfloat16),
@@ -105,8 +109,8 @@
                 [((i + 4 * step) % count, i) for i in range(count)],
             )
         )
-    lent = lax.ppermute((near[1] + mlp(mate, *second)).astype(jnp.bfloat16), "col", mates)
-    mixed = near[0] + mlp(home, *second) + lent.astype(jnp.float32)
+    lent = lax.ppermute(near[1].astype(jnp.bfloat16), "col", mates)
+    mixed = near[0] + lent.astype(jnp.float32)
     for part in back:
         mixed = mixed + part.astype(jnp.float32)
     result = grid.astype(jnp.float32) + layer_scale * (mixed + b_out)

time: 342 us -> 261 us (0.76); the launches traced: 337 us -> 261 us
  waiting for transfers between devices: 173 us -> 106 us
  matrix products: 92.7 us -> 61.1 us
  between operations: 0.65 us -> 13.7 us
  starting transfers between devices: 28.1 us -> 34.9 us
    ppermute x4 -> x2, waiting for transfers between devices: 80.3 us -> 3.19 us  [the longest x1 3.19 us: local(): other = lax.ppermute(b_in, 'col', sides)]
    dot_general x8, matrix products: 89.7 us -> 58 us  [the longest x4 44.7 us: expand(): lax.dot_general(rows, weight_rows, (((1,), (1,)), ((), ())), preferred_el...]
    all_gather x0 -> x2, waiting for transfers between devices: none -> 14.7 us  [local(): lax.all_gather(part, 'col', axis=0, tiled=True, axis_index_groups=groups)]
    ppermute x1, starting transfers between devices: 7.56 us -> 18.9 us  [local(): lax.ppermute(flat, 'col', [(i, (i + 4 * step) % count) for i in range(cou...]
    ppermute x4 -> x2, starting transfers between devices: 5.61 us -> 0.86 us  [the longest x1 0.5 us: local(): lent = lax.ppermute(near[1].astype(jnp.bfloat16), 'col', mates)]
    ppermute x1, waiting for transfers between devices: 26 us -> 22 us  [local(): lax.ppermute(total.astype(jnp.bfloat16), 'col', [((i + 4 * step) % count,...]
  transfers between devices with their start and end apart: 14 -> 14, of which waited for: 8 -> 8; matrix products, arithmetic and copies ran while one was open for 20% -> 34% of each run, Pallas kernels for 0% -> 0%
where the time goes in v3:
time: 261 us
  waiting for transfers between devices  106 us (41%)
  matrix products  61.1 us (23%)
  starting transfers between devices  34.9 us (13%)
  other arithmetic  32.3 us (12%)
  between operations  13.7 us (5%)
  blocking collectives  9.62 us (4%)
    dot_general x4, matrix products, expand(): lax.dot_general(rows, weight_rows, (((1,), (1,)), ((), ())), preferred_el...  44.7 us
    ppermute x1, waiting for transfers between devices, local(): lax.ppermute(flat, 'col', [(i, (i + 4 * step) % count) for i in range(cou...  30.5 us
    all_to_all x1, waiting for transfers between devices, local(): lax.all_to_all(patches, 'col', split_axis=0, concat_axis=0, tiled=True)  27.9 us
    reduce_sum x1, other arithmetic, local(): mean = jnp.mean(conv, axis=-1, keepdims=True)  26.2 us
    ppermute x1, waiting for transfers between devices, local(): lax.ppermute(total.astype(jnp.bfloat16), 'col', [((i + 4 * step) % count,...  22 us
    ppermute x1, starting transfers between devices, local(): lax.ppermute(flat, 'col', [(i, (i + 4 * step) % count) for i in range(cou...  18.9 us
    all_gather x2, waiting for transfers between devices, local(): lax.all_gather(part, 'col', axis=0, tiled=True, axis_index_groups=groups)  14.7 us
    dot_general x4, matrix products, mlp(): return jnp.dot(hidden, weight_out, preferred_element_type=jnp.float32)  13.3 us
  transfers between devices with their start and end apart: 14, of which 8 were waited for; matrix products, arithmetic and copies ran while one was open for 34% of the time, Pallas kernels for 0%

profile of v3, /device:TPU:0, one launch (start us, length us, event | category | flops | bytes accessed | tf_op | source)
XLA Modules:
  0.0 260.6 jit_solution(6969405985337579008)
XLA Ops:
  6.5 0.8 all_to_all.14
  7.3 9.6 %all_to_all.21 = s32[8,96,1]{1,2,0:T(1,128)S(1)} all-to-all(s32[8,96,1]{1,2,0:T(1,128)S(1)} %bitcast.35), channel_id=1, replica_groups=mesh['row'=4,'col'=8] {'col'}, dimensions={0} | all-to-all | bytes 6144 | tf_op jit(solution)/shard_map/all_to_all | solution.py:70
  16.9 4.4 %all-to-all-start.1 = ((bf16[8,96,1536]{2,1,0:T(8,128)(2,1)}), bf16[8,96,1536]{2,1,0:T(8,128)(2,1)}, u32[]{:S(2)}, u32[]{:S(2)}) async-start(bf16[8,96,1536]{2,1,0:T(8,128)(2,1)} %bitcast.29), calls=%async_computation.1 | async-start | bytes 4718592 | tf_op jit(solution)/shard_map/all_to_all | solution.py:69
  21.3 0.0 all-gather.3.cloned.1.call-start
  21.3 0.5 broadcast.323
  21.9 0.7 reduce.101
  22.5 0.1 eq.17
  22.6 0.3 fusion.45
  22.9 27.9 %all-to-all-done.1 = bf16[8,96,1536]{2,1,0:T(8,128)(2,1)} async-done(((bf16[8,96,1536]{2,1,0:T(8,128)(2,1)}), bf16[8,96,1536]{2,1,0:T(8,128)(2,1)}, u32[]{:S(2)}, u32[]{:S(2)}) %all-to-all-start.1) | async-done | bytes 2359328 | tf_op jit(solution)/shard_map/all_to_all | solution.py:69
  50.8 3.0 %fusion.40 = bf16[512,1536]{1,0:T(8,128)(2,1)S(1)} fusion(bf16[768,1536]{1,0:T(8,128)(2,1)} %bitcast.2, bf16[1536]{0:T(1024)(128)(2,1)S(1)} %copy-done.9, pred[512]{0:T(512)(128)(4,1)S(1)} %fusion.45, s32[768]{0:T(1024)S(1)} %eq.17), kind=kOutput, calls=%fused_computation.86 | convolution fusion | flops 1209139200 | bytes 3938816 | tf_op jit(solution)/shard_map/dot_general | solution.py:74
  53.9 3.6 %collective-permute-start = (bf16[3,16,1536]{2,1,0:T(8,128)(2,1)S(1)}, bf16[3,16,1536]{2,1,0:T(8,128)(2,1)S(1)}, u32[]{:S(2)}, u32[]{:S(2)}) collective-permute-start(bf16[3,16,1536]{2,1,0:T(8,128)(2,1)S(1)} %bitcast.34), channel_id=1, source_target_pairs={{0,8},{8,16},{16,24},{1,9},{9,17},{17,25},{2,10},{10,18},{18,26},{... | collective-permute-start | bytes 442376 | tf_op jit(solution)/shard_map/ppermute | solution.py:18
  57.5 1.3 collective-permute-start.1
  58.8 0.0 all-gather.3.cloned.1.call-update
  58.8 0.0 all-gather.5.cloned.1.call-start
  58.9 1.3 collective-permute-done
  60.1 4.4 %collective-permute-done.1 = bf16[3,16,1536]{2,1,0:T(8,128)(2,1)S(1)} collective-permute-done((bf16[3,16,1536]{2,1,0:T(8,128)(2,1)S(1)}, bf16[3,16,1536]{2,1,0:T(8,128)(2,1)S(1)}, u32[]{:S(2)}, u32[]{:S(2)}) %collective-permute-start.1) | collective-permute-done | bytes 147488 | tf_op jit(solution)/shard_map/ppermute | solution.py:20
  64.5 0.4 pad_maximum_fusion.5
  64.9 1.3 collective-permute-start.2
  66.2 1.5 collective-permute-start.3
  67.7 0.2 slice_reduce_fusion.46
  67.9 0.3 slice_reduce_fusion.48
  68.2 0.3 slice_reduce_fusion.47
  68.6 2.5 collective-permute-done.3
  71.1 1.6 maximum_maximum_fusion
  72.7 26.2 %fusion.47 = (f32[32,16]{1,0:T(8,128)S(1)}, f32[32,16,1536]{2,1,0:T(8,128)S(1)}) fusion(f32[1536]{0:T(1024)S(1)} %get-tuple-element.52, bf16[38,19,1536]{2,1,0:T(8,128)(2,1)S(1)} %get-tuple-element.57, f32[1536]{0:T(1024)S(1)} %get-tuple-element.53, f32[1536]{0:T(1024)S(1)} %get-tuple-element.6, f32[1536]{0:T(1024)S(1)} %get-tuple-element.7, ...), kind=kLoop, calls=%fused_computation.165 | loop fusion | flops 121110016 | bytes 71383040 | tf_op jit(solution)/shard_map/reduce_sum | solution.py:89
  98.9 0.4 multiply_reduce_fusion
  99.4 0.2 copy-done.2
  99.6 0.6 add_convert_fusion.2
  100.2 18.9 %collective-permute-start.7 = (bf16[512,1536]{1,0:T(8,128)(2,1)S(1)}, bf16[512,1536]{1,0:T(8,128)(2,1)}, u32[]{:S(2)}, u32[]{:S(2)}) collective-permute-start(bf16[512,1536]{1,0:T(8,128)(2,1)S(1)} %bitcast.30), channel_id=1, source_target_pairs={{0,4},{1,5},{2,6},{3,7},{4,0},{5,1},{6,2},{7,3},{8,12},{9,13},{10,... | collective-permute-start | bytes 4718600 | tf_op jit(solution)/shard_map/ppermute | solution.py:97
  119.1 0.4 collective-permute-start.4
  119.6 3.2 %collective-permute-done.4 = bf16[768]{0:T(1024)(128)(2,1)S(1)} collective-permute-done((bf16[768]{0:T(1024)(128)(2,1)S(1)}, bf16[768]{0:T(1024)(128)(2,1)S(1)}, u32[]{:S(2)}, u32[]{:S(2)}) %collective-permute-start.4) | collective-permute-done | bytes 1568 | tf_op jit(solution)/shard_map/ppermute | solution.py:64
  122.8 0.4 collective-permute-start.5
  123.1 30.5 %collective-permute-done.7 = bf16[512,1536]{1,0:T(8,128)(2,1)} collective-permute-done((bf16[512,1536]{1,0:T(8,128)(2,1)S(1)}, bf16[512,1536]{1,0:T(8,128)(2,1)}, u32[]{:S(2)}, u32[]{:S(2)}) %collective-permute-start.7) | collective-permute-done | bytes 1572896 | tf_op jit(solution)/shard_map/ppermute | solution.py:97
  153.7 1.0 collective-permute-start.8
  154.6 12.4 %fusion.8 = bf16[512,1536]{1,0:T(8,128)(2,1)} fusion(bf16[512,1536]{1,0:T(8,128)(2,1)} %collective-permute-done.7, bf16[1536,1536]{1,0:T(8,128)(2,1)} %all-gather.3.cloned.1.call-done, f32[1536]{0:T(1024)S(1)} %maximum_convert_fusion), kind=kOutput, calls=%fused_computation.17 | convolution fusion | flops 2467823616 | bytes 7870464 | tf_op jit(solution)/shard_map/dot_general | solution.py:28
  167.0 11.7 %fusion.11 = bf16[512,1536]{1,0:T(8,128)(2,1)} fusion(bf16[512,1536]{1,0:T(8,128)(2,1)} %collective-permute-done.8, bf16[1536,1536]{1,0:T(8,128)(2,1)S(1)} %copy-done.7, f32[1536]{0:T(1024)S(1)} %maximum_convert_fusion), kind=kOutput, calls=%fused_computation.20 | convolution fusion | flops 2467823616 | bytes 7870464 | tf_op jit(solution)/shard_map/dot_general | solution.py:28
  178.7 14.7 %all-gather.5.cloned.1.call-done = bf16[1536,1536]{1,0:T(8,128)(2,1)} async-done(((bf16[768,1536]{1,0:T(8,128)(2,1)}), bf16[1536,1536]{1,0:T(8,128)(2,1)}) %all-gather.5.cloned.1.call-update) | async-done | bytes 4718608 | tf_op jit(solution)/shard_map/all_gather | solution.py:61
  193.3 5.6 %convolution_convert_fusion = bf16[512,1536]{1,0:T(8,128)(2,1)S(1)} fusion(bf16[512,1536]{1,0:T(8,128)(2,1)} %fusion.11, bf16[1536,1536]{1,0:T(8,128)(2,1)} %all-gather.5.cloned.1.call-done), kind=kOutput, calls=%fused_computation.87 | convolution fusion | flops 2416705536 | bytes 7864320 | tf_op jit(solution)/shard_map/dot_general | solution.py:36
  198.9 0.1 collective-permute-start.9
  199.0 10.4 %fusion.5 = bf16[512,1536]{1,0:T(8,128)(2,1)S(1)} fusion(bf16[512,1536]{1,0:T(8,128)(2,1)} %collective-permute-done.5, bf16[1536,1536]{1,0:T(8,128)(2,1)S(1)} %copy-done.8, f32[1536]{0:T(1024)S(1)} %maximum_convert_fusion), kind=kOutput, calls=%fused_computation.14 | convolution fusion | flops 2467823616 | bytes 7870464 | tf_op jit(solution)/shard_map/dot_general | solution.py:28
  209.4 2.6 convolution_convert_fusion.1
  212.0 0.5 collective-permute-start.6
  212.5 2.6 add_convert_fusion.1
  215.1 1.5 collective-permute-start.10
  216.7 10.2 %fusion.2 = bf16[512,1536]{1,0:T(8,128)(2,1)S(1)} fusion(bf16[512,1536]{1,0:T(8,128)(2,1)S(1)} %bitcast.32, bf16[1536,1536]{1,0:T(8,128)(2,1)S(1)} %copy-done.8, f32[1536]{0:T(1024)S(1)} %maximum_convert_fusion), kind=kOutput, calls=%fused_computation.11 | convolution fusion | flops 2467823616 | bytes 7870464 | tf_op jit(solution)/shard_map/dot_general | solution.py:28
  227.0 2.6 fusion.49
  229.6 22.0 %collective-permute-done.10 = bf16[512,1536]{1,0:T(8,128)(2,1)S(1)} collective-permute-done((bf16[512,1536]{1,0:T(8,128)(2,1)S(1)}, bf16[512,1536]{1,0:T(8,128)(2,1)S(1)}, u32[]{:S(2)}, u32[]{:S(2)}) %collective-permute-start.10) | collective-permute-done | bytes 1572896 | tf_op jit(solution)/shard_map/ppermute | solution.py:106
  251.6 2.2 add_convert_fusion
  (38 shorter events, 0.2 us)
Async XLA Ops:
  6.5 44.2 %copy-start.9 = (bf16[1536]{0:T(1024)(128)(2,1)S(1)}, bf16[1536]{0:T(1024)(128)(2,1)}, u32[]{:S(2)}) copy-start(bf16[1536]{0:T(1024)(128)(2,1)} %param.14) | copy-start | bytes 9220
  16.9 33.8 %all-to-all-start.1 = ((bf16[8,96,1536]{2,1,0:T(8,128)(2,1)}), bf16[8,96,1536]{2,1,0:T(8,128)(2,1)}, u32[]{:S(2)}, u32[]{:S(2)}) async-start(bf16[8,96,1536]{2,1,0:T(8,128)(2,1)} %bitcast.29), calls=%async_computation.1 | async-start | bytes 4718592 | tf_op jit(solution)/shard_map/all_to_all | solution.py:69
  21.3 133.3 %all-gather.3.cloned.1.call-start = ((), (), s32[]{:S(2)}) async-start(), calls=%async_computation.2 | async-start | bytes 7077888 | tf_op jit(solution)/shard_map/all_gather | solution.py:61
  53.8 13.9 %copy-start = (f32[7,7,1536]{2,1,0:T(8,128)S(1)}, f32[7,7,1536]{2,1,0:T(8,128)}, u32[]{:S(2)}) copy-start(f32[7,7,1536]{2,1,0:T(8,128)} %param.15) | copy-start | bytes 903172
  53.9 6.3 %collective-permute-start = (bf16[3,16,1536]{2,1,0:T(8,128)(2,1)S(1)}, bf16[3,16,1536]{2,1,0:T(8,128)(2,1)S(1)}, u32[]{:S(2)}, u32[]{:S(2)}) collective-permute-start(bf16[3,16,1536]{2,1,0:T(8,128)(2,1)S(1)} %bitcast.34), channel_id=1, source_target_pairs={{0,8},{8,16},{16,24},{1,9},{9,17},{17,25},{2,10},{10,18},{18,26},{... | collective-permute-start | bytes 442376 | tf_op jit(solution)/shard_map/ppermute | solution.py:18
  57.5 7.0 %collective-permute-start.1 = (bf16[3,16,1536]{2,1,0:T(8,128)(2,1)S(1)}, bf16[3,16,1536]{2,1,0:T(8,128)(2,1)S(1)}, u32[]{:S(2)}, u32[]{:S(2)}) collective-permute-start(bf16[3,16,1536]{2,1,0:T(8,128)(2,1)S(1)} %bitcast.33), channel_id=1, source_target_pairs={{8,0},{16,8},{24,16},{9,1},{17,9},{25,17},{10,2},{18,10},{26,18},{... | collective-permute-start | bytes 442376 | tf_op jit(solution)/shard_map/ppermute | solution.py:20
  58.8 134.5 %all-gather.5.cloned.1.call-start = ((), (), s32[]{:S(2)}) async-start(), calls=%async_computation.3 | async-start | bytes 7077888 | tf_op jit(solution)/shard_map/all_gather | solution.py:61
  64.9 3.7 %collective-permute-start.2 = (bf16[38,3,1536]{2,1,0:T(4,128)(2,1)S(1)}, bf16[38,3,1536]{2,1,0:T(4,128)(2,1)S(1)}, u32[]{:S(2)}, u32[]{:S(2)}) collective-permute-start(bf16[38,3,1536]{2,1,0:T(4,128)(2,1)S(1)} %get-tuple-element.58), channel_id=1, source_target_pairs={{0,1},{1,2},{2,3},{3,4},{4,5},{5,6},{6,7},{8,9},{9,10},{10,11},{11... | collective-permute-start | bytes 1050632 | tf_op jit(solution)/shard_map/ppermute | solution.py:18
  66.2 4.8 %collective-permute-start.3 = (bf16[38,3,1536]{2,1,0:T(4,128)(2,1)S(1)}, bf16[38,3,1536]{2,1,0:T(4,128)(2,1)S(1)}, u32[]{:S(2)}, u32[]{:S(2)}) collective-permute-start(bf16[38,3,1536]{2,1,0:T(4,128)(2,1)S(1)} %get-tuple-element.59), channel_id=1, source_target_pairs={{1,0},{2,1},{3,2},{4,3},{5,4},{6,5},{7,6},{9,8},{10,9},{11,10},{12... | collective-permute-start | bytes 1050632 | tf_op jit(solution)/shard_map/ppermute | solution.py:20
  68.6 4.1 %copy-start.1 = (f32[1536]{0:T(1024)S(1)}, f32[1536]{0:T(1024)}, u32[]{:S(2)}) copy-start(f32[1536]{0:T(1024)} %param.16) | copy-start | bytes 18436
  98.9 0.7 copy-start.2
  98.9 0.7 copy-start.3
  99.4 19.8 %copy-start.6 = (bf16[768]{0:T(1024)(128)(2,1)S(1)}, bf16[768]{0:T(1024)(128)(2,1)}, u32[]{:S(2)}) copy-start(bf16[768]{0:T(1024)(128)(2,1)} %param.20) | copy-start | bytes 4612
  100.2 53.4 %collective-permute-start.7 = (bf16[512,1536]{1,0:T(8,128)(2,1)S(1)}, bf16[512,1536]{1,0:T(8,128)(2,1)}, u32[]{:S(2)}, u32[]{:S(2)}) collective-permute-start(bf16[512,1536]{1,0:T(8,128)(2,1)S(1)} %bitcast.30), channel_id=1, source_target_pairs={{0,4},{1,5},{2,6},{3,7},{4,0},{5,1},{6,2},{7,3},{8,12},{9,13},{10,... | collective-permute-start | bytes 4718600 | tf_op jit(solution)/shard_map/ppermute | solution.py:97
  119.1 3.6 %collective-permute-start.4 = (bf16[768]{0:T(1024)(128)(2,1)S(1)}, bf16[768]{0:T(1024)(128)(2,1)S(1)}, u32[]{:S(2)}, u32[]{:S(2)}) collective-permute-start(bf16[768]{0:T(1024)(128)(2,1)S(1)} %copy-done.6), channel_id=1, source_target_pairs={{0,2},{1,3},{2,0},{3,1},{4,6},{5,7},{6,4},{7,5},{8,10},{9,11},{10,... | collective-permute-start | bytes 4616 | tf_op jit(solution)/shard_map/ppermute | solution.py:64
  122.8 76.2 %collective-permute-start.5 = (bf16[512,1536]{1,0:T(8,128)(2,1)S(1)}, bf16[512,1536]{1,0:T(8,128)(2,1)}, u32[]{:S(2)}, u32[]{:S(2)}) collective-permute-start(bf16[512,1536]{1,0:T(8,128)(2,1)S(1)} %bitcast.31), channel_id=1, source_target_pairs={{0,1},{1,0},{2,3},{3,2},{4,5},{5,4},{6,7},{7,6},{8,9},{9,8},{10,11... | collective-permute-start | bytes 4718600 | tf_op jit(solution)/shard_map/ppermute | solution.py:94
  153.7 13.3 %collective-permute-start.8 = (bf16[512,1536]{1,0:T(8,128)(2,1)}, bf16[512,1536]{1,0:T(8,128)(2,1)}, u32[]{:S(2)}, u32[]{:S(2)}) collective-permute-start(bf16[512,1536]{1,0:T(8,128)(2,1)} %collective-permute-done.7), channel_id=1, source_target_pairs={{0,1},{1,0},{2,3},{3,2},{4,5},{5,4},{6,7},{7,6},{8,9},{9,8},{10,11... | collective-permute-start | bytes 4718600 | tf_op jit(solution)/shard_map/ppermute | solution.py:98
  154.6 12.4 %copy-start.7 = (bf16[1536,1536]{1,0:T(8,128)(2,1)S(1)}, bf16[1536,1536]{1,0:T(8,128)(2,1)}, u32[]{:S(2)}) copy-start(bf16[1536,1536]{1,0:T(8,128)(2,1)} %all-gather.3.cloned.1.call-done) | copy-start | bytes 14155780
  193.3 5.7 %copy-start.8 = (bf16[1536,1536]{1,0:T(8,128)(2,1)S(1)}, bf16[1536,1536]{1,0:T(8,128)(2,1)}, u32[]{:S(2)}) copy-start(bf16[1536,1536]{1,0:T(8,128)(2,1)} %all-gather.3.cloned.1.call-done) | copy-start | bytes 14155780
  193.3 16.1 %slice-start = ((s8[4718592]{0:T(1024)(128)(4,1)}), s8[4194304]{0:T(1024)(128)(4,1)S(1)}, s32[]{:S(2)}) async-start(s8[4718592]{0:T(1024)(128)(4,1)} %bitcast.36), calls=%async_computation.4 | async-start | bytes 8388608
  198.9 10.5 %slice-start.1 = ((s8[4718592]{0:T(1024)(128)(4,1)}), s8[524288]{0:T(1024)(128)(4,1)S(1)}, s32[]{:S(2)}) async-start(s8[4718592]{0:T(1024)(128)(4,1)} %bitcast.36), calls=%async_computation.5 | async-start | bytes 1048576
  198.9 13.6 %collective-permute-start.9 = (bf16[512,1536]{1,0:T(8,128)(2,1)S(1)}, bf16[512,1536]{1,0:T(8,128)(2,1)S(1)}, u32[]{:S(2)}, u32[]{:S(2)}) collective-permute-start(bf16[512,1536]{1,0:T(8,128)(2,1)S(1)} %convolution_convert_fusion), channel_id=1, source_target_pairs={{0,1},{1,0},{2,3},{3,2},{4,5},{5,4},{6,7},{7,6},{8,9},{9,8},{10,11... | collective-permute-start | bytes 4718600 | tf_op jit(solution)/shard_map/ppermute | solution.py:103
  209.4 3.1 %copy-start.10 = (bf16[512,1536]{1,0:T(8,128)(2,1)S(1)}, bf16[512,1536]{1,0:T(8,128)(2,1)}, u32[]{:S(2)}) copy-start(bf16[512,1536]{1,0:T(8,128)(2,1)} %fusion.8) | copy-start | bytes 4718596
  212.0 17.5 %collective-permute-start.6 = (bf16[512,1536]{1,0:T(8,128)(2,1)S(1)}, bf16[512,1536]{1,0:T(8,128)(2,1)S(1)}, u32[]{:S(2)}, u32[]{:S(2)}) collective-permute-start(bf16[512,1536]{1,0:T(8,128)(2,1)S(1)} %convolution_convert_fusion.1), channel_id=1, source_target_pairs={{0,1},{1,0},{2,3},{3,2},{4,5},{5,4},{6,7},{7,6},{8,9},{9,8},{10,11... | collective-permute-start | bytes 4718600 | tf_op jit(solution)/shard_map/ppermute | solution.py:112
  215.1 36.4 %collective-permute-start.10 = (bf16[512,1536]{1,0:T(8,128)(2,1)S(1)}, bf16[512,1536]{1,0:T(8,128)(2,1)S(1)}, u32[]{:S(2)}, u32[]{:S(2)}) collective-permute-start(bf16[512,1536]{1,0:T(8,128)(2,1)S(1)} %add_convert_fusion.1), channel_id=1, source_target_pairs={{4,0},{5,1},{6,2},{7,3},{0,4},{1,5},{2,6},{3,7},{12,8},{13,9},{14,... | collective-permute-start | bytes 4718600 | tf_op jit(solution)/shard_map/ppermute | solution.py:106
  226.9 24.7 %copy-start.4 = (f32[1536]{0:T(1024)S(1)}, f32[1536]{0:T(1024)}, u32[]{:S(2)}) copy-start(f32[1536]{0:T(1024)} %param.22) | copy-start | bytes 18436
  226.9 24.6 %copy-start.5 = (f32[1536]{0:T(1024)S(1)}, f32[1536]{0:T(1024)}, u32[]{:S(2)}) copy-start(f32[1536]{0:T(1024)} %param.23) | copy-start | bytes 18436
Sparse Core Ops, SparseCore 0:
  58.9 71.6 all-gather.2
  132.2 61.1 all-gather.4

commit v4 on v3

--- a/solution.py
+++ b/solution.py
@@ -57,9 +57,8 @@
     mates = [(i, i ^ 1) for i in range(count)]
     sides = [(i, i ^ 2) for i in range(count)]
     groups = [[i, i ^ 2] for i in range(count) if i % 4 < 2]
-    pair_in, pair_out = (
-        lax.all_gather(part, "col", axis=0, tiled=True, axis_index_groups=groups)
-        for part in (w_in, w_out)
+    pair_in, pair_out = lax.all_gather(
+        jnp.stack([w_in, w_out]), "col", axis=1, tiled=True, axis_index_groups=groups
     )
     other = lax.ppermute(b_in, "col", sides)
     low = lax.axis_index("col") % 4 < 2
@@ -92,11 +91,13 @@
     normed = (centred * lax.rsqrt(var + 1e-06) * norm_gain + norm_bias).astype(jnp.bfloat16)
     flat = normed.reshape(cells, channels)
     home, mate = flat, lax.ppermute(flat, "col", mates)
+    near = [mlp(home, *pair)]
     away = []
     for step in range(1, lines):
         there = lax.ppermute(flat, "col", [(i, (i + 4 * step) % count) for i in range(count)])
+        there, near[0] = lax.optimization_barrier((there, near[0]))
         away.append((there, lax.ppermute(there, "col", mates)))
-    near = [mlp(home, *pair), mlp(mate, *pair)]
+    near.append(mlp(mate, *pair))
     back = []
     for step, (there, cross) in enumerate(away, 1):
         lent = mlp(cross, *pair).astype(jnp.bfloat16)

time: 261 us -> 262 us (level)
  other arithmetic: 32.3 us -> 39.4 us
  waiting for transfers between devices: 106 us -> 101 us
  matrix products: 61.1 us -> 56.6 us
    ppermute x1, waiting for transfers between devices: 30.5 us -> 0.01 us  [local(): lax.ppermute(flat, 'col', [(i, (i + 4 * step) % count) for i in range(cou...]
    ppermute x1, starting transfers between devices: 0.36 us -> 21.2 us  [local(): home, mate = (flat, lax.ppermute(flat, 'col', mates))]
    all_gather x2 -> x1, waiting for transfers between devices: 14.7 us -> 34.3 us  [local(): lax.all_gather(jnp.stack([w_in, w_out]), 'col', axis=1, tiled=True, axis_...]
    ppermute x1, starting transfers between devices: 18.9 us -> 0.55 us  [local(): lax.ppermute(flat, 'col', [(i, (i + 4 * step) % count) for i in range(cou...]
    ppermute x1, waiting for transfers between devices: 22 us -> 36.1 us  [local(): lax.ppermute(total.astype(jnp.bfloat16), 'col', [((i + 4 * step) % count,...]
    ppermute x2, waiting for transfers between devices: 6.86 us -> 0.04 us  [extended(): lax.ppermute(head, axis, [((i + 1) % count, i) for i in range(ends)])]
    another operation x0 -> x1, other arithmetic: none -> 5.04 us  [local(): jnp.stack([w_in, w_out])]
    ppermute x1, waiting for transfers between devices: 3.19 us -> 0.01 us  [local(): other = lax.ppermute(b_in, 'col', sides)]
  transfers between devices with their start and end apart: 14 -> 13, of which waited for: 8 -> 5; matrix products, arithmetic and copies ran while one was open for 34% -> 37% of each run, Pallas kernels for 0% -> 0%
where the time goes in v4:
time: 262 us; the launch traced here: 261 us
  waiting for transfers between devices  101 us (39%)
  matrix products  56.6 us (22%)
  other arithmetic  39.4 us (15%)
  starting transfers between devices  37.5 us (14%)
  between operations  13.9 us (5%)
  blocking collectives  9.62 us (4%)
  local copies, waits for them, and re-layouts  3.68 us (1%)
    dot_general x4, matrix products, expand(): lax.dot_general(rows, weight_rows, (((1,), (1,)), ((), ())), preferred_el...  43.1 us
    ppermute x1, waiting for transfers between devices, local(): lax.ppermute(total.astype(jnp.bfloat16), 'col', [((i + 4 * step) % count,...  36.1 us
    all_gather x1, waiting for transfers between devices, local(): lax.all_gather(jnp.stack([w_in, w_out]), 'col', axis=1, tiled=True, axis_...  34.3 us
    all_to_all x1, waiting for transfers between devices, local(): lax.all_to_all(patches, 'col', split_axis=0, concat_axis=0, tiled=True)  28.2 us
    reduce_sum x1, other arithmetic, local(): mean = jnp.mean(conv, axis=-1, keepdims=True)  26.2 us
    ppermute x1, starting transfers between devices, local(): home, mate = (flat, lax.ppermute(flat, 'col', mates))  21.2 us
    dot_general x4, matrix products, mlp(): return jnp.dot(hidden, weight_out, preferred_element_type=jnp.float32)  10.4 us
    all_to_all x1, blocking collectives, local(): lax.all_to_all(dest, 'col', split_axis=0, concat_axis=0, tiled=True)  9.62 us
  transfers between devices with their start and end apart: 13, of which 5 were waited for; matrix products, arithmetic and copies ran while one was open for 37% of the time, Pallas kernels for 0%

profile of v4, /device:TPU:0, one launch (start us, length us, event | category | flops | bytes accessed | tf_op | source)
XLA Modules:
  0.0 261.1 jit_solution(3914920805779693093)
XLA Ops:
  6.5 0.8 all_to_all.14
  7.3 9.6 %all_to_all.21 = s32[8,96,1]{1,2,0:T(1,128)S(1)} all-to-all(s32[8,96,1]{1,2,0:T(1,128)S(1)} %bitcast.49), channel_id=1, replica_groups=mesh['row'=4,'col'=8] {'col'}, dimensions={0} | all-to-all | bytes 6144 | tf_op jit(solution)/shard_map/all_to_all | solution.py:69
  16.9 4.4 %all-to-all-start.1 = ((bf16[8,96,1536]{2,1,0:T(8,128)(2,1)}), bf16[8,96,1536]{2,1,0:T(8,128)(2,1)}, u32[]{:S(2)}, u32[]{:S(2)}) async-start(bf16[8,96,1536]{2,1,0:T(8,128)(2,1)} %bitcast.41), calls=%async_computation.1 | async-start | bytes 4718592 | tf_op jit(solution)/shard_map/all_to_all | solution.py:68
  21.3 0.0 all-gather.2.cloned.1.call-start
  21.3 5.0 %pad_maximum_fusion = bf16[2,768,1536]{2,1,0:T(8,128)(2,1)} fusion(bf16[1,768,1536]{2,1,0:T(8,128)(2,1)} %bitcast.42, bf16[1,768,1536]{2,1,0:T(8,128)(2,1)} %bitcast.43), kind=kLoop, calls=%fused_computation.6 | loop fusion | flops 2359296 | bytes 9437184 | tf_op jit(solution)/shard_map/stack | solution.py:61
  26.4 0.0 all-gather.2.cloned.1.call-update
  26.4 1.9 collective-permute-start.5
  28.3 0.5 broadcast.323
  28.8 0.7 reduce.101
  29.5 0.1 eq.17
  29.6 0.3 fusion.51
  29.8 28.2 %all-to-all-done.1 = bf16[8,96,1536]{2,1,0:T(8,128)(2,1)} async-done(((bf16[8,96,1536]{2,1,0:T(8,128)(2,1)}), bf16[8,96,1536]{2,1,0:T(8,128)(2,1)}, u32[]{:S(2)}, u32[]{:S(2)}) %all-to-all-start.1) | async-done | bytes 2359328 | tf_op jit(solution)/shard_map/all_to_all | solution.py:68
  58.1 3.1 %fusion.46 = bf16[512,1536]{1,0:T(8,128)(2,1)S(1)} fusion(bf16[768,1536]{1,0:T(8,128)(2,1)} %bitcast.2, bf16[1536]{0:T(1024)(128)(2,1)S(1)} %copy-done.22, pred[512]{0:T(512)(128)(4,1)S(1)} %fusion.51, s32[768]{0:T(1024)S(1)} %eq.17), kind=kOutput, calls=%fused_computation.95 | convolution fusion | flops 1209139200 | bytes 3938816 | tf_op jit(solution)/shard_map/dot_general | solution.py:73
  61.2 1.3 collective-permute-start.1
  62.5 4.6 %collective-permute-start = (bf16[3,16,1536]{2,1,0:T(8,128)(2,1)S(1)}, bf16[3,16,1536]{2,1,0:T(8,128)(2,1)S(1)}, u32[]{:S(2)}, u32[]{:S(2)}) collective-permute-start(bf16[3,16,1536]{2,1,0:T(8,128)(2,1)S(1)} %bitcast.47), channel_id=1, source_target_pairs={{0,8},{8,16},{16,24},{1,9},{9,17},{17,25},{2,10},{10,18},{18,26},{... | collective-permute-start | bytes 442376 | tf_op jit(solution)/shard_map/ppermute | solution.py:18
  67.1 0.3 slice_reduce_fusion.48
  67.4 0.9 slice_reduce_fusion.47
  68.3 1.4 collective-permute-done
  69.7 1.1 pad_maximum_fusion.6
  70.8 1.3 collective-permute-start.2
  72.2 1.5 collective-permute-start.3
  73.6 0.8 slice_reduce_fusion.46
  74.4 0.7 broadcast_select_fusion.1
  75.1 0.6 maximum_convert_fusion
  75.8 0.0 collective-permute-done.3
  75.9 1.6 maximum_maximum_fusion
  77.7 26.2 %fusion.53 = (f32[32,16]{1,0:T(8,128)S(1)}, f32[32,16,1536]{2,1,0:T(8,128)S(1)}) fusion(f32[1536]{0:T(1024)S(1)} %copy-done.13, bf16[38,19,1536]{2,1,0:T(8,128)(2,1)S(1)} %get-tuple-element.61, f32[1536]{0:T(1024)S(1)} %copy-done.14, f32[1536]{0:T(1024)S(1)} %get-tuple-element.10, f32[1536]{0:T(1024)S(1)} %get-tuple-element.11, ...), kind=kLoop, calls=%fused_computation.172 | loop fusion | flops 121110016 | bytes 71383040 | tf_op jit(solution)/shard_map/reduce_sum | solution.py:88
  103.9 0.4 multiply_reduce_fusion
  104.3 0.2 copy-done.16
  104.6 0.6 add_convert_fusion.2
  105.1 21.2 %collective-permute-start.6 = (bf16[512,1536]{1,0:T(8,128)(2,1)S(1)}, bf16[512,1536]{1,0:T(8,128)(2,1)}, u32[]{:S(2)}, u32[]{:S(2)}) collective-permute-start(bf16[512,1536]{1,0:T(8,128)(2,1)S(1)} %bitcast.44), channel_id=1, source_target_pairs={{0,1},{1,0},{2,3},{3,2},{4,5},{5,4},{6,7},{7,6},{8,9},{9,8},{10,11... | collective-permute-start | bytes 4718600 | tf_op jit(solution)/shard_map/ppermute | solution.py:93
  126.3 0.6 collective-permute-start.4
  126.8 34.3 %all-gather.2.cloned.1.call-done = bf16[2,1536,1536]{2,1,0:T(8,128)(2,1)} async-done(((bf16[2,768,1536]{2,1,0:T(8,128)(2,1)}), bf16[2,1536,1536]{2,1,0:T(8,128)(2,1)}) %all-gather.2.cloned.1.call-update) | async-done | bytes 9437200 | tf_op jit(solution)/shard_map/all_gather | solution.py:60
  161.1 11.1 %fusion.2 = bf16[512,1536]{1,0:T(8,128)(2,1)S(1)} fusion(bf16[512,1536]{1,0:T(8,128)(2,1)S(1)} %bitcast.46, bf16[2,1536,1536]{2,1,0:T(8,128)(2,1)} %all-gather.2.cloned.1.call-done, f32[1536]{0:T(1024)S(1)} %copy-done.20), kind=kOutput, calls=%fused_computation.14 | convolution fusion | flops 2467823616 | bytes 7870464 | tf_op jit(solution)/shard_map/dot_general | solution.py:28
  172.3 2.6 fusion.43
  174.9 0.1 collective-permute-start.8
  175.0 11.0 %fusion.8 = bf16[512,1536]{1,0:T(8,128)(2,1)S(1)} fusion(bf16[512,1536]{1,0:T(8,128)(2,1)} %collective-permute-done.4, bf16[2,1536,1536]{2,1,0:T(8,128)(2,1)S(1)} %copy-done.21, f32[1536]{0:T(1024)S(1)} %copy-done.20), kind=kOutput, calls=%fused_computation.20 | convolution fusion | flops 2467823616 | bytes 7872512 | tf_op jit(solution)/shard_map/dot_general | solution.py:28
  186.1 9.8 %fusion.11 = bf16[512,1536]{1,0:T(8,128)(2,1)S(1)} fusion(bf16[512,1536]{1,0:T(8,128)(2,1)S(1)} %collective-permute-done.8, bf16[2,1536,1536]{2,1,0:T(8,128)(2,1)S(1)} %copy-done.21, f32[1536]{0:T(1024)S(1)} %copy-done.20), kind=kOutput, calls=%fused_computation.23 | convolution fusion | flops 2467823616 | bytes 7872512 | tf_op jit(solution)/shard_map/dot_general | solution.py:28
  195.9 2.6 fusion.45
  198.5 0.3 collective-permute-start.9
  198.8 11.1 %fusion.5 = bf16[512,1536]{1,0:T(8,128)(2,1)S(1)} fusion(bf16[512,1536]{1,0:T(8,128)(2,1)} %collective-permute-done.6, bf16[2,1536,1536]{2,1,0:T(8,128)(2,1)S(1)} %copy-done.21, f32[1536]{0:T(1024)S(1)} %copy-done.20), kind=kOutput, calls=%fused_computation.17 | convolution fusion | flops 2467823616 | bytes 7872512 | tf_op jit(solution)/shard_map/dot_general | solution.py:28
  209.9 2.6 fusion.44
  212.6 0.3 collective-permute-start.7
  212.9 2.6 add_convert_fusion.1
  215.5 0.1 collective-permute-start.10
  215.6 0.5 collective-permute-done.7
  216.0 36.1 %collective-permute-done.10 = bf16[512,1536]{1,0:T(8,128)(2,1)S(1)} collective-permute-done((bf16[512,1536]{1,0:T(8,128)(2,1)S(1)}, bf16[512,1536]{1,0:T(8,128)(2,1)S(1)}, u32[]{:S(2)}, u32[]{:S(2)}) %collective-permute-start.10) | collective-permute-done | bytes 1572896 | tf_op jit(solution)/shard_map/ppermute | solution.py:107
  252.1 2.2 add_convert_fusion
  (55 shorter events, 0.2 us)
Async XLA Ops:
  16.9 41.2 %all-to-all-start.1 = ((bf16[8,96,1536]{2,1,0:T(8,128)(2,1)}), bf16[8,96,1536]{2,1,0:T(8,128)(2,1)}, u32[]{:S(2)}, u32[]{:S(2)}) async-start(bf16[8,96,1536]{2,1,0:T(8,128)(2,1)} %bitcast.41), calls=%async_computation.1 | async-start | bytes 4718592 | tf_op jit(solution)/shard_map/all_to_all | solution.py:68
  21.3 139.9 %all-gather.2.cloned.1.call-start = ((), (), s32[]{:S(2)}) async-start(), calls=%async_computation.2 | async-start | bytes 14155776 | tf_op jit(solution)/shard_map/all_gather | solution.py:60
  26.4 31.7 %copy-start.22 = (bf16[1536]{0:T(1024)(128)(2,1)S(1)}, bf16[1536]{0:T(1024)(128)(2,1)}, u32[]{:S(2)}) copy-start(bf16[1536]{0:T(1024)(128)(2,1)} %param.14) | copy-start | bytes 9220
  26.4 48.0 %collective-permute-start.5 = (bf16[768]{0:T(1024)(128)(2,1)}, bf16[768]{0:T(1024)(128)(2,1)}, u32[]{:S(2)}, u32[]{:S(2)}) collective-permute-start(bf16[768]{0:T(1024)(128)(2,1)} %param.20), channel_id=1, source_target_pairs={{0,2},{1,3},{2,0},{3,1},{4,6},{5,7},{6,4},{7,5},{8,10},{9,11},{10,... | collective-permute-start | bytes 4616 | tf_op jit(solution)/shard_map/ppermute | solution.py:63
  58.1 9.0 %copy-start = (f32[7,7,1536]{2,1,0:T(8,128)S(1)}, f32[7,7,1536]{2,1,0:T(8,128)}, u32[]{:S(2)}) copy-start(f32[7,7,1536]{2,1,0:T(8,128)} %param.15) | copy-start | bytes 903172
  61.2 7.1 %collective-permute-start.1 = (bf16[3,16,1536]{2,1,0:T(8,128)(2,1)S(1)}, bf16[3,16,1536]{2,1,0:T(8,128)(2,1)S(1)}, u32[]{:S(2)}, u32[]{:S(2)}) collective-permute-start(bf16[3,16,1536]{2,1,0:T(8,128)(2,1)S(1)} %bitcast.48), channel_id=1, source_target_pairs={{8,0},{16,8},{24,16},{9,1},{17,9},{25,17},{10,2},{18,10},{26,18},{... | collective-permute-start | bytes 442376 | tf_op jit(solution)/shard_map/ppermute | solution.py:20
  62.5 7.2 %collective-permute-start = (bf16[3,16,1536]{2,1,0:T(8,128)(2,1)S(1)}, bf16[3,16,1536]{2,1,0:T(8,128)(2,1)S(1)}, u32[]{:S(2)}, u32[]{:S(2)}) collective-permute-start(bf16[3,16,1536]{2,1,0:T(8,128)(2,1)S(1)} %bitcast.47), channel_id=1, source_target_pairs={{0,8},{8,16},{16,24},{1,9},{9,17},{17,25},{2,10},{10,18},{18,26},{... | collective-permute-start | bytes 442376 | tf_op jit(solution)/shard_map/ppermute | solution.py:18
  70.8 5.0 %collective-permute-start.2 = (bf16[38,3,1536]{2,1,0:T(4,128)(2,1)}, bf16[38,3,1536]{2,1,0:T(4,128)(2,1)S(1)}, u32[]{:S(2)}, u32[]{:S(2)}) collective-permute-start(bf16[38,3,1536]{2,1,0:T(4,128)(2,1)} %get-tuple-element.62), channel_id=1, source_target_pairs={{0,1},{1,2},{2,3},{3,4},{4,5},{5,6},{6,7},{8,9},{9,10},{10,11},{11... | collective-permute-start | bytes 1050632 | tf_op jit(solution)/shard_map/ppermute | solution.py:18
  72.2 3.7 %collective-permute-start.3 = (bf16[38,3,1536]{2,1,0:T(4,128)(2,1)S(1)}, bf16[38,3,1536]{2,1,0:T(4,128)(2,1)S(1)}, u32[]{:S(2)}, u32[]{:S(2)}) collective-permute-start(bf16[38,3,1536]{2,1,0:T(4,128)(2,1)S(1)} %get-tuple-element.63), channel_id=1, source_target_pairs={{1,0},{2,1},{3,2},{4,3},{5,4},{6,5},{7,6},{9,8},{10,9},{11,10},{12... | collective-permute-start | bytes 1050632 | tf_op jit(solution)/shard_map/ppermute | solution.py:20
  75.7 1.8 copy-start.1
  75.7 1.8 copy-start.2
  75.7 1.8 copy-start.3
  75.7 1.8 copy-start.4
  75.7 1.8 copy-start.5
  75.7 1.8 copy-start.6
  75.7 1.8 copy-start.7
  75.8 1.8 copy-start.8
  75.8 1.8 copy-start.9
  75.8 1.8 copy-start.10
  75.8 1.8 copy-start.11
  75.8 1.8 copy-start.12
  75.8 1.8 copy-start.13
  75.8 1.8 copy-start.14
  75.8 1.8 copy-start.15
  103.8 0.7 copy-start.16
  103.8 0.7 copy-start.17
  104.3 56.8 %copy-start.20 = (f32[1536]{0:T(1024)S(1)}, f32[1536]{0:T(1024)}, u32[]{:S(2)}) copy-start(f32[1536]{0:T(1024)} %maximum_convert_fusion) | copy-start | bytes 18436
  105.1 93.7 %collective-permute-start.6 = (bf16[512,1536]{1,0:T(8,128)(2,1)S(1)}, bf16[512,1536]{1,0:T(8,128)(2,1)}, u32[]{:S(2)}, u32[]{:S(2)}) collective-permute-start(bf16[512,1536]{1,0:T(8,128)(2,1)S(1)} %bitcast.44), channel_id=1, source_target_pairs={{0,1},{1,0},{2,3},{3,2},{4,5},{5,4},{6,7},{7,6},{8,9},{9,8},{10,11... | collective-permute-start | bytes 4718600 | tf_op jit(solution)/shard_map/ppermute | solution.py:93
  126.3 48.6 %collective-permute-start.4 = (bf16[512,1536]{1,0:T(8,128)(2,1)S(1)}, bf16[512,1536]{1,0:T(8,128)(2,1)}, u32[]{:S(2)}, u32[]{:S(2)}) collective-permute-start(bf16[512,1536]{1,0:T(8,128)(2,1)S(1)} %bitcast.45), channel_id=1, source_target_pairs={{0,4},{1,5},{2,6},{3,7},{4,0},{5,1},{6,2},{7,3},{8,12},{9,13},{10,... | collective-permute-start | bytes 4718600 | tf_op jit(solution)/shard_map/ppermute | solution.py:97
  161.1 11.1 %copy-start.21 = (bf16[2,1536,1536]{2,1,0:T(8,128)(2,1)S(1)}, bf16[2,1536,1536]{2,1,0:T(8,128)(2,1)}, u32[]{:S(2)}) copy-start(bf16[2,1536,1536]{2,1,0:T(8,128)(2,1)} %all-gather.2.cloned.1.call-done) | copy-start | bytes 28311556
  174.9 11.2 %collective-permute-start.8 = (bf16[512,1536]{1,0:T(8,128)(2,1)}, bf16[512,1536]{1,0:T(8,128)(2,1)S(1)}, u32[]{:S(2)}, u32[]{:S(2)}) collective-permute-start(bf16[512,1536]{1,0:T(8,128)(2,1)} %collective-permute-done.4), channel_id=1, source_target_pairs={{0,1},{1,0},{2,3},{3,2},{4,5},{5,4},{6,7},{7,6},{8,9},{9,8},{10,11... | collective-permute-start | bytes 4718600 | tf_op jit(solution)/shard_map/ppermute | solution.py:99
  198.5 14.4 %collective-permute-start.9 = (bf16[512,1536]{1,0:T(8,128)(2,1)S(1)}, bf16[512,1536]{1,0:T(8,128)(2,1)S(1)}, u32[]{:S(2)}, u32[]{:S(2)}) collective-permute-start(bf16[512,1536]{1,0:T(8,128)(2,1)S(1)} %fusion.45), channel_id=1, source_target_pairs={{0,1},{1,0},{2,3},{3,2},{4,5},{5,4},{6,7},{7,6},{8,9},{9,8},{10,11... | collective-permute-start | bytes 4718600 | tf_op jit(solution)/shard_map/ppermute | solution.py:104
  212.5 39.6 %copy-start.18 = (f32[1536]{0:T(1024)S(1)}, f32[1536]{0:T(1024)}, u32[]{:S(2)}) copy-start(f32[1536]{0:T(1024)} %param.22) | copy-start | bytes 18436
  212.6 39.6 %copy-start.19 = (f32[1536]{0:T(1024)S(1)}, f32[1536]{0:T(1024)}, u32[]{:S(2)}) copy-start(f32[1536]{0:T(1024)} %param.23) | copy-start | bytes 18436
  212.6 3.5 %collective-permute-start.7 = (bf16[512,1536]{1,0:T(8,128)(2,1)S(1)}, bf16[512,1536]{1,0:T(8,128)(2,1)S(1)}, u32[]{:S(2)}, u32[]{:S(2)}) collective-permute-start(bf16[512,1536]{1,0:T(8,128)(2,1)S(1)} %fusion.44), channel_id=1, source_target_pairs={{0,1},{1,0},{2,3},{3,2},{4,5},{5,4},{6,7},{7,6},{8,9},{9,8},{10,11... | collective-permute-start | bytes 4718600 | tf_op jit(solution)/shard_map/ppermute | solution.py:113
  215.5 36.6 %collective-permute-start.10 = (bf16[512,1536]{1,0:T(8,128)(2,1)S(1)}, bf16[512,1536]{1,0:T(8,128)(2,1)S(1)}, u32[]{:S(2)}, u32[]{:S(2)}) collective-permute-start(bf16[512,1536]{1,0:T(8,128)(2,1)S(1)} %add_convert_fusion.1), channel_id=1, source_target_pairs={{4,0},{5,1},{6,2},{7,3},{0,4},{1,5},{2,6},{3,7},{12,8},{13,9},{14,... | collective-permute-start | bytes 4718600 | tf_op jit(solution)/shard_map/ppermute | solution.py:107
Sparse Core Ops, SparseCore 0:
  26.5 134.5 all-gather.1

commit v5 on v4

--- a/solution.py
+++ b/solution.py
@@ -91,27 +91,26 @@
     normed = (centred * lax.rsqrt(var + 1e-06) * norm_gain + norm_bias).astype(jnp.bfloat16)
     flat = normed.reshape(cells, channels)
     home, mate = flat, lax.ppermute(flat, "col", mates)
-    near = [mlp(home, *pair)]
     away = []
     for step in range(1, lines):
         there = lax.ppermute(flat, "col", [(i, (i + 4 * step) % count) for i in range(count)])
-        there, near[0] = lax.optimization_barrier((there, near[0]))
         away.append((there, lax.ppermute(there, "col", mates)))
-    near.append(mlp(mate, *pair))
+    near = mlp(mate, *pair)
     back = []
     for step, (there, cross) in enumerate(away, 1):
         lent = mlp(cross, *pair).astype(jnp.bfloat16)
         lent = lax.ppermute(lent, "col", mates)
         total = mlp(there, *pair) + lent.astype(jnp.float32)
+        total, home = lax.optimization_barrier((total.astype(jnp.bfloat16), home))
         back.append(
             lax.ppermute(
-                total.astype(jnp.bfloat16),
+                total,
                 "col",
                 [((i + 4 * step) % count, i) for i in range(count)],
             )
         )
-    lent = lax.ppermute(near[1].astype(jnp.bfloat16), "col", mates)
-    mixed = near[0] + lent.astype(jnp.float32)
+    lent = lax.ppermute(near.astype(jnp.bfloat16), "col", mates)
+    mixed = mlp(home, *pair) + lent.astype(jnp.float32)
     for part in back:
         mixed = mixed + part.astype(jnp.float32)
     result = grid.astype(jnp.float32) + layer_scale * (mixed + b_out)

time: 262 us -> 267 us (1.019)
  waiting for transfers between devices: 101 us -> 119 us
  starting transfers between devices: 37.5 us -> 29.5 us
  other arithmetic: 39.4 us -> 35 us
    ppermute x1, waiting for transfers between devices: 0.01 us -> 32.2 us  [local(): lax.ppermute(flat, 'col', [(i, (i + 4 * step) % count) for i in range(cou...]
    ppermute x1, starting transfers between devices: 21.2 us -> 0.1 us  [local(): home, mate = (flat, lax.ppermute(flat, 'col', mates))]
    ppermute x2, waiting for transfers between devices: 36.5 us -> 24 us  [the longest x1 24 us: local(): lax.ppermute(total, 'col', [((i + 4 * step) % count, i) for i in range(co...]
    ppermute x1, starting transfers between devices: 0.55 us -> 9.88 us  [local(): lax.ppermute(flat, 'col', [(i, (i + 4 * step) % count) for i in range(cou...]
    ppermute x1, starting transfers between devices: 0.12 us -> 3.28 us  [local(): away.append((there, lax.ppermute(there, 'col', mates)))]
    all_gather x1, waiting for transfers between devices: 34.3 us -> 31.3 us  [local(): lax.all_gather(jnp.stack([w_in, w_out]), 'col', axis=1, tiled=True, axis_...]
  transfers between devices with their start and end apart: 13 -> 13, of which waited for: 5 -> 6; matrix products, arithmetic and copies ran while one was open for 37% -> 33% of each run, Pallas kernels for 0% -> 0%
where the time goes in v5:
time: 267 us
  waiting for transfers between devices  119 us (45%)
  matrix products  56.8 us (21%)
  other arithmetic  35 us (13%)
  starting transfers between devices  29.5 us (11%)
  between operations  13.7 us (5%)
  blocking collectives  9.62 us (4%)
    dot_general x4, matrix products, expand(): lax.dot_general(rows, weight_rows, (((1,), (1,)), ((), ())), preferred_el...  43.1 us
    ppermute x1, waiting for transfers between devices, local(): lax.ppermute(flat, 'col', [(i, (i + 4 * step) % count) for i in range(cou...  32.2 us
    all_gather x1, waiting for transfers between devices, local(): lax.all_gather(jnp.stack([w_in, w_out]), 'col', axis=1, tiled=True, axis_...  31.3 us
    all_to_all x1, waiting for transfers between devices, local(): lax.all_to_all(patches, 'col', split_axis=0, concat_axis=0, tiled=True)  27.9 us
    reduce_sum x1, other arithmetic, local(): mean = jnp.mean(conv, axis=-1, keepdims=True)  26.2 us
    ppermute x1, waiting for transfers between devices, local(): lax.ppermute(total, 'col', [((i + 4 * step) % count, i) for i in range(co...  24 us
    dot_general x4, matrix products, mlp(): return jnp.dot(hidden, weight_out, preferred_element_type=jnp.float32)  10.5 us
    ppermute x1, starting transfers between devices, local(): lax.ppermute(flat, 'col', [(i, (i + 4 * step) % count) for i in range(cou...  9.88 us
  transfers between devices with their start and end apart: 13, of which 6 were waited for; matrix products, arithmetic and copies ran while one was open for 33% of the time, Pallas kernels for 0%

profile of v5, /device:TPU:0, one launch (start us, length us, event | category | flops | bytes accessed | tf_op | source)
XLA Modules:
  0.0 266.5 jit_solution(9492926077718082232)
XLA Ops:
  6.5 0.8 all_to_all.14
  7.3 9.6 %all_to_all.21 = s32[8,96,1]{1,2,0:T(1,128)S(1)} all-to-all(s32[8,96,1]{1,2,0:T(1,128)S(1)} %bitcast.49), channel_id=1, replica_groups=mesh['row'=4,'col'=8] {'col'}, dimensions={0} | all-to-all | bytes 6144 | tf_op jit(solution)/shard_map/all_to_all | solution.py:69
  16.9 4.4 %all-to-all-start.1 = ((bf16[8,96,1536]{2,1,0:T(8,128)(2,1)}), bf16[8,96,1536]{2,1,0:T(8,128)(2,1)}, u32[]{:S(2)}, u32[]{:S(2)}) async-start(bf16[8,96,1536]{2,1,0:T(8,128)(2,1)} %bitcast.41), calls=%async_computation.1 | async-start | bytes 4718592 | tf_op jit(solution)/shard_map/all_to_all | solution.py:68
  21.3 0.0 all-gather.2.cloned.1.call-start
  21.3 0.5 broadcast.323
  21.9 0.7 reduce.101
  22.5 0.1 eq.17
  22.6 0.3 fusion.51
  22.9 27.9 %all-to-all-done.1 = bf16[8,96,1536]{2,1,0:T(8,128)(2,1)} async-done(((bf16[8,96,1536]{2,1,0:T(8,128)(2,1)}), bf16[8,96,1536]{2,1,0:T(8,128)(2,1)}, u32[]{:S(2)}, u32[]{:S(2)}) %all-to-all-start.1) | async-done | bytes 2359328 | tf_op jit(solution)/shard_map/all_to_all | solution.py:68
  50.8 3.2 %fusion.46 = bf16[512,1536]{1,0:T(8,128)(2,1)S(1)} fusion(bf16[768,1536]{1,0:T(8,128)(2,1)} %bitcast.2, bf16[1536]{0:T(1024)(128)(2,1)S(1)} %copy-done.10, pred[512]{0:T(512)(128)(4,1)S(1)} %fusion.51, s32[768]{0:T(1024)S(1)} %eq.17), kind=kOutput, calls=%fused_computation.95 | convolution fusion | flops 1209139200 | bytes 3938816 | tf_op jit(solution)/shard_map/dot_general | solution.py:73
  54.0 1.3 collective-permute-start.1
  55.3 4.6 %collective-permute-start = (bf16[3,16,1536]{2,1,0:T(8,128)(2,1)S(1)}, bf16[3,16,1536]{2,1,0:T(8,128)(2,1)S(1)}, u32[]{:S(2)}, u32[]{:S(2)}) collective-permute-start(bf16[3,16,1536]{2,1,0:T(8,128)(2,1)S(1)} %bitcast.47), channel_id=1, source_target_pairs={{0,8},{8,16},{16,24},{1,9},{9,17},{17,25},{2,10},{10,18},{18,26},{... | collective-permute-start | bytes 442376 | tf_op jit(solution)/shard_map/ppermute | solution.py:18
  59.9 2.6 pad_maximum_fusion
  62.5 0.0 all-gather.2.cloned.1.call-update
  62.6 0.4 pad_maximum_fusion.6
  63.0 1.3 collective-permute-start.2
  64.3 1.5 collective-permute-start.3
  65.8 0.2 slice_reduce_fusion.46
  66.0 0.3 slice_reduce_fusion.48
  66.3 0.3 slice_reduce_fusion.47
  66.6 2.4 collective-permute-done.3
  69.0 1.6 maximum_maximum_fusion
  70.7 26.2 %fusion.53 = (f32[32,16]{1,0:T(8,128)S(1)}, f32[32,16,1536]{2,1,0:T(8,128)S(1)}) fusion(f32[1536]{0:T(1024)S(1)} %get-tuple-element.56, bf16[38,19,1536]{2,1,0:T(8,128)(2,1)S(1)} %get-tuple-element.61, f32[1536]{0:T(1024)S(1)} %get-tuple-element.57, f32[1536]{0:T(1024)S(1)} %get-tuple-element.10, f32[1536]{0:T(1024)S(1)} %get-tuple-element.11, ...), kind=kLoop, calls=%fused_computation.172 | loop fusion | flops 121110016 | bytes 71383040 | tf_op jit(solution)/shard_map/reduce_sum | solution.py:88
  96.9 0.0 copy-start.4
  96.9 0.4 multiply_reduce_fusion
  97.4 0.2 copy-done.4
  97.6 0.0 copy-done.5
  97.6 0.6 add_convert_fusion.2
  98.2 9.9 %collective-permute-start.4 = (bf16[512,1536]{1,0:T(8,128)(2,1)S(1)}, bf16[512,1536]{1,0:T(8,128)(2,1)}, u32[]{:S(2)}, u32[]{:S(2)}) collective-permute-start(bf16[512,1536]{1,0:T(8,128)(2,1)S(1)} %bitcast.44), channel_id=1, source_target_pairs={{0,4},{1,5},{2,6},{3,7},{4,0},{5,1},{6,2},{7,3},{8,12},{9,13},{10,... | collective-permute-start | bytes 4718600 | tf_op jit(solution)/shard_map/ppermute | solution.py:96
  108.1 32.2 %collective-permute-done.4 = bf16[512,1536]{1,0:T(8,128)(2,1)} collective-permute-done((bf16[512,1536]{1,0:T(8,128)(2,1)S(1)}, bf16[512,1536]{1,0:T(8,128)(2,1)}, u32[]{:S(2)}, u32[]{:S(2)}) %collective-permute-start.4) | collective-permute-done | bytes 1572896 | tf_op jit(solution)/shard_map/ppermute | solution.py:96
  140.3 3.3 %collective-permute-start.6 = (bf16[512,1536]{1,0:T(8,128)(2,1)}, bf16[512,1536]{1,0:T(8,128)(2,1)}, u32[]{:S(2)}, u32[]{:S(2)}) collective-permute-start(bf16[512,1536]{1,0:T(8,128)(2,1)} %collective-permute-done.4), channel_id=1, source_target_pairs={{0,1},{1,0},{2,3},{3,2},{4,5},{5,4},{6,7},{7,6},{8,9},{9,8},{10,11... | collective-permute-start | bytes 4718600 | tf_op jit(solution)/shard_map/ppermute | solution.py:97
  143.6 2.7 %collective-permute-start.5 = (bf16[768]{0:T(1024)(128)(2,1)S(1)}, bf16[768]{0:T(1024)(128)(2,1)S(1)}, u32[]{:S(2)}, u32[]{:S(2)}) collective-permute-start(bf16[768]{0:T(1024)(128)(2,1)S(1)} %copy-done.8), channel_id=1, source_target_pairs={{0,2},{1,3},{2,0},{3,1},{4,6},{5,7},{6,4},{7,5},{8,10},{9,11},{10,... | collective-permute-start | bytes 4616 | tf_op jit(solution)/shard_map/ppermute | solution.py:63
  146.2 1.6 collective-permute-done.5
  147.8 0.1 collective-permute-start.8
  147.9 31.3 %all-gather.2.cloned.1.call-done = bf16[2,1536,1536]{2,1,0:T(8,128)(2,1)} async-done(((bf16[2,768,1536]{2,1,0:T(8,128)(2,1)}), bf16[2,1536,1536]{2,1,0:T(8,128)(2,1)}) %all-gather.2.cloned.1.call-update) | async-done | bytes 9437200 | tf_op jit(solution)/shard_map/all_gather | solution.py:60
  179.2 11.4 %fusion.5 = bf16[512,1536]{1,0:T(8,128)(2,1)S(1)} fusion(bf16[512,1536]{1,0:T(8,128)(2,1)} %collective-permute-done.6, bf16[2,1536,1536]{2,1,0:T(8,128)(2,1)} %all-gather.2.cloned.1.call-done, f32[1536]{0:T(1024)S(1)} %maximum_convert_fusion), kind=kOutput, calls=%fused_computation.17 | convolution fusion | flops 2467823616 | bytes 7870464 | tf_op jit(solution)/shard_map/dot_general | solution.py:28
  190.6 2.6 fusion.44
  193.3 0.1 collective-permute-start.7
  193.4 11.0 %fusion.2 = bf16[512,1536]{1,0:T(8,128)(2,1)S(1)} fusion(bf16[512,1536]{1,0:T(8,128)(2,1)} %collective-permute-done.4, bf16[2,1536,1536]{2,1,0:T(8,128)(2,1)S(1)} %copy-done.9, f32[1536]{0:T(1024)S(1)} %maximum_convert_fusion), kind=kOutput, calls=%fused_computation.14 | convolution fusion | flops 2467823616 | bytes 7872512 | tf_op jit(solution)/shard_map/dot_general | solution.py:28
  204.4 10.9 %fusion.11 = bf16[512,1536]{1,0:T(8,128)(2,1)S(1)} fusion(bf16[512,1536]{1,0:T(8,128)(2,1)} %collective-permute-done.8, bf16[2,1536,1536]{2,1,0:T(8,128)(2,1)S(1)} %copy-done.9, f32[1536]{0:T(1024)S(1)} %maximum_convert_fusion), kind=kOutput, calls=%fused_computation.23 | convolution fusion | flops 2467823616 | bytes 7872512 | tf_op jit(solution)/shard_map/dot_general | solution.py:28
  215.3 2.6 fusion.45
  218.0 0.3 collective-permute-start.9
  218.3 2.6 add_convert_fusion.1
  220.9 0.1 collective-permute-start.10
  221.0 9.8 %fusion.8 = bf16[512,1536]{1,0:T(8,128)(2,1)S(1)} fusion(bf16[512,1536]{1,0:T(8,128)(2,1)S(1)} %bitcast.46, bf16[2,1536,1536]{2,1,0:T(8,128)(2,1)S(1)} %copy-done.9, f32[1536]{0:T(1024)S(1)} %maximum_convert_fusion), kind=kOutput, calls=%fused_computation.20 | convolution fusion | flops 2467823616 | bytes 7872512 | tf_op jit(solution)/shard_map/dot_general | solution.py:28
  230.8 2.6 fusion.41
  233.5 24.0 %collective-permute-done.10 = bf16[512,1536]{1,0:T(8,128)(2,1)S(1)} collective-permute-done((bf16[512,1536]{1,0:T(8,128)(2,1)S(1)}, bf16[512,1536]{1,0:T(8,128)(2,1)S(1)}, u32[]{:S(2)}, u32[]{:S(2)}) %collective-permute-start.10) | collective-permute-done | bytes 1572896 | tf_op jit(solution)/shard_map/ppermute | solution.py:106
  257.5 2.2 add_convert_fusion
  (31 shorter events, 0.1 us)
Async XLA Ops:
  6.5 44.2 %copy-start.10 = (bf16[1536]{0:T(1024)(128)(2,1)S(1)}, bf16[1536]{0:T(1024)(128)(2,1)}, u32[]{:S(2)}) copy-start(bf16[1536]{0:T(1024)(128)(2,1)} %param.14) | copy-start | bytes 9220
  16.9 33.8 %all-to-all-start.1 = ((bf16[8,96,1536]{2,1,0:T(8,128)(2,1)}), bf16[8,96,1536]{2,1,0:T(8,128)(2,1)}, u32[]{:S(2)}, u32[]{:S(2)}) async-start(bf16[8,96,1536]{2,1,0:T(8,128)(2,1)} %bitcast.41), calls=%async_computation.1 | async-start | bytes 4718592 | tf_op jit(solution)/shard_map/all_to_all | solution.py:68
  21.3 157.9 %all-gather.2.cloned.1.call-start = ((), (), s32[]{:S(2)}) async-start(), calls=%async_computation.2 | async-start | bytes 14155776 | tf_op jit(solution)/shard_map/all_gather | solution.py:60
  50.8 9.1 %copy-start = (bf16[768,1536]{1,0:T(8,128)(2,1)S(1)}, bf16[768,1536]{1,0:T(8,128)(2,1)}, u32[]{:S(2)}) copy-start(bf16[768,1536]{1,0:T(8,128)(2,1)} %param.21) | copy-start | bytes 7077892
  50.8 9.1 %copy-start.1 = (bf16[768,1536]{1,0:T(8,128)(2,1)S(1)}, bf16[768,1536]{1,0:T(8,128)(2,1)}, u32[]{:S(2)}) copy-start(bf16[768,1536]{1,0:T(8,128)(2,1)} %param.19) | copy-start | bytes 7077892
  54.0 8.6 %collective-permute-start.1 = (bf16[3,16,1536]{2,1,0:T(8,128)(2,1)S(1)}, bf16[3,16,1536]{2,1,0:T(8,128)(2,1)S(1)}, u32[]{:S(2)}, u32[]{:S(2)}) collective-permute-start(bf16[3,16,1536]{2,1,0:T(8,128)(2,1)S(1)} %bitcast.48), channel_id=1, source_target_pairs={{8,0},{16,8},{24,16},{9,1},{17,9},{25,17},{10,2},{18,10},{26,18},{... | collective-permute-start | bytes 442376 | tf_op jit(solution)/shard_map/ppermute | solution.py:20
  55.3 7.3 %collective-permute-start = (bf16[3,16,1536]{2,1,0:T(8,128)(2,1)S(1)}, bf16[3,16,1536]{2,1,0:T(8,128)(2,1)S(1)}, u32[]{:S(2)}, u32[]{:S(2)}) collective-permute-start(bf16[3,16,1536]{2,1,0:T(8,128)(2,1)S(1)} %bitcast.47), channel_id=1, source_target_pairs={{0,8},{8,16},{16,24},{1,9},{9,17},{17,25},{2,10},{10,18},{18,26},{... | collective-permute-start | bytes 442376 | tf_op jit(solution)/shard_map/ppermute | solution.py:18
  62.5 3.2 %copy-start.2 = (f32[7,7,1536]{2,1,0:T(8,128)S(1)}, f32[7,7,1536]{2,1,0:T(8,128)}, u32[]{:S(2)}) copy-start(f32[7,7,1536]{2,1,0:T(8,128)} %param.15) | copy-start | bytes 903172
  63.0 3.7 %collective-permute-start.2 = (bf16[38,3,1536]{2,1,0:T(4,128)(2,1)S(1)}, bf16[38,3,1536]{2,1,0:T(4,128)(2,1)S(1)}, u32[]{:S(2)}, u32[]{:S(2)}) collective-permute-start(bf16[38,3,1536]{2,1,0:T(4,128)(2,1)S(1)} %get-tuple-element.62), channel_id=1, source_target_pairs={{0,1},{1,2},{2,3},{3,4},{4,5},{5,6},{6,7},{8,9},{9,10},{10,11},{11... | collective-permute-start | bytes 1050632 | tf_op jit(solution)/shard_map/ppermute | solution.py:18
  64.3 4.7 %collective-permute-start.3 = (bf16[38,3,1536]{2,1,0:T(4,128)(2,1)S(1)}, bf16[38,3,1536]{2,1,0:T(4,128)(2,1)S(1)}, u32[]{:S(2)}, u32[]{:S(2)}) collective-permute-start(bf16[38,3,1536]{2,1,0:T(4,128)(2,1)S(1)} %get-tuple-element.63), channel_id=1, source_target_pairs={{1,0},{2,1},{3,2},{4,3},{5,4},{6,5},{7,6},{9,8},{10,9},{11,10},{12... | collective-permute-start | bytes 1050632 | tf_op jit(solution)/shard_map/ppermute | solution.py:20
  66.6 4.1 %copy-start.3 = (f32[1536]{0:T(1024)S(1)}, f32[1536]{0:T(1024)}, u32[]{:S(2)}) copy-start(f32[1536]{0:T(1024)} %param.16) | copy-start | bytes 18436
  96.9 0.7 copy-start.4
  96.9 0.7 copy-start.5
  97.4 46.2 %copy-start.8 = (bf16[768]{0:T(1024)(128)(2,1)S(1)}, bf16[768]{0:T(1024)(128)(2,1)}, u32[]{:S(2)}) copy-start(bf16[768]{0:T(1024)(128)(2,1)} %param.20) | copy-start | bytes 4612
  98.2 42.1 %collective-permute-start.4 = (bf16[512,1536]{1,0:T(8,128)(2,1)S(1)}, bf16[512,1536]{1,0:T(8,128)(2,1)}, u32[]{:S(2)}, u32[]{:S(2)}) collective-permute-start(bf16[512,1536]{1,0:T(8,128)(2,1)S(1)} %bitcast.44), channel_id=1, source_target_pairs={{0,4},{1,5},{2,6},{3,7},{4,0},{5,1},{6,2},{7,3},{8,12},{9,13},{10,... | collective-permute-start | bytes 4718600 | tf_op jit(solution)/shard_map/ppermute | solution.py:96
  140.3 7.7 %collective-permute-start.6 = (bf16[512,1536]{1,0:T(8,128)(2,1)}, bf16[512,1536]{1,0:T(8,128)(2,1)}, u32[]{:S(2)}, u32[]{:S(2)}) collective-permute-start(bf16[512,1536]{1,0:T(8,128)(2,1)} %collective-permute-done.4), channel_id=1, source_target_pairs={{0,1},{1,0},{2,3},{3,2},{4,5},{5,4},{6,7},{7,6},{8,9},{9,8},{10,11... | collective-permute-start | bytes 4718600 | tf_op jit(solution)/shard_map/ppermute | solution.py:97
  143.6 4.3 %collective-permute-start.5 = (bf16[768]{0:T(1024)(128)(2,1)S(1)}, bf16[768]{0:T(1024)(128)(2,1)S(1)}, u32[]{:S(2)}, u32[]{:S(2)}) collective-permute-start(bf16[768]{0:T(1024)(128)(2,1)S(1)} %copy-done.8), channel_id=1, source_target_pairs={{0,2},{1,3},{2,0},{3,1},{4,6},{5,7},{6,4},{7,5},{8,10},{9,11},{10,... | collective-permute-start | bytes 4616 | tf_op jit(solution)/shard_map/ppermute | solution.py:63
  147.8 56.6 %collective-permute-start.8 = (bf16[512,1536]{1,0:T(8,128)(2,1)S(1)}, bf16[512,1536]{1,0:T(8,128)(2,1)}, u32[]{:S(2)}, u32[]{:S(2)}) collective-permute-start(bf16[512,1536]{1,0:T(8,128)(2,1)S(1)} %bitcast.45), channel_id=1, source_target_pairs={{0,1},{1,0},{2,3},{3,2},{4,5},{5,4},{6,7},{7,6},{8,9},{9,8},{10,11... | collective-permute-start | bytes 4718600 | tf_op jit(solution)/shard_map/ppermute | solution.py:93
  179.2 11.4 %copy-start.9 = (bf16[2,1536,1536]{2,1,0:T(8,128)(2,1)S(1)}, bf16[2,1536,1536]{2,1,0:T(8,128)(2,1)}, u32[]{:S(2)}) copy-start(bf16[2,1536,1536]{2,1,0:T(8,128)(2,1)} %all-gather.2.cloned.1.call-done) | copy-start | bytes 28311556
  193.3 25.0 %collective-permute-start.7 = (bf16[512,1536]{1,0:T(8,128)(2,1)S(1)}, bf16[512,1536]{1,0:T(8,128)(2,1)S(1)}, u32[]{:S(2)}, u32[]{:S(2)}) collective-permute-start(bf16[512,1536]{1,0:T(8,128)(2,1)S(1)} %fusion.44), channel_id=1, source_target_pairs={{0,1},{1,0},{2,3},{3,2},{4,5},{5,4},{6,7},{7,6},{8,9},{9,8},{10,11... | collective-permute-start | bytes 4718600 | tf_op jit(solution)/shard_map/ppermute | solution.py:102
  218.0 15.5 %collective-permute-start.9 = (bf16[512,1536]{1,0:T(8,128)(2,1)S(1)}, bf16[512,1536]{1,0:T(8,128)(2,1)S(1)}, u32[]{:S(2)}, u32[]{:S(2)}) collective-permute-start(bf16[512,1536]{1,0:T(8,128)(2,1)S(1)} %fusion.45), channel_id=1, source_target_pairs={{0,1},{1,0},{2,3},{3,2},{4,5},{5,4},{6,7},{7,6},{8,9},{9,8},{10,11... | collective-permute-start | bytes 4718600 | tf_op jit(solution)/shard_map/ppermute | solution.py:112
  220.9 36.6 %collective-permute-start.10 = (bf16[512,1536]{1,0:T(8,128)(2,1)S(1)}, bf16[512,1536]{1,0:T(8,128)(2,1)S(1)}, u32[]{:S(2)}, u32[]{:S(2)}) collective-permute-start(bf16[512,1536]{1,0:T(8,128)(2,1)S(1)} %add_convert_fusion.1), channel_id=1, source_target_pairs={{4,0},{5,1},{6,2},{7,3},{0,4},{1,5},{2,6},{3,7},{12,8},{13,9},{14,... | collective-permute-start | bytes 4718600 | tf_op jit(solution)/shard_map/ppermute | solution.py:106
  230.8 26.7 %copy-start.6 = (f32[1536]{0:T(1024)S(1)}, f32[1536]{0:T(1024)}, u32[]{:S(2)}) copy-start(f32[1536]{0:T(1024)} %param.22) | copy-start | bytes 18436
  230.8 26.7 %copy-start.7 = (f32[1536]{0:T(1024)S(1)}, f32[1536]{0:T(1024)}, u32[]{:S(2)}) copy-start(f32[1536]{0:T(1024)} %param.23) | copy-start | bytes 18436
Sparse Core Ops, SparseCore 0:
  62.7 116.5 all-gather.1

commit v6 on v5

--- a/solution.py
+++ b/solution.py
@@ -57,8 +57,9 @@
     mates = [(i, i ^ 1) for i in range(count)]
     sides = [(i, i ^ 2) for i in range(count)]
     groups = [[i, i ^ 2] for i in range(count) if i % 4 < 2]
-    pair_in, pair_out = lax.all_gather(
-        jnp.stack([w_in, w_out]), "col", axis=1, tiled=True, axis_index_groups=groups
+    pair_in, pair_out = (
+        lax.all_gather(part, "col", axis=0, tiled=True, axis_index_groups=groups)
+        for part in (w_in, w_out)
     )
     other = lax.ppermute(b_in, "col", sides)
     low = lax.axis_index("col") % 4 < 2

time: 267 us -> 261 us (0.978)
  waiting for transfers between devices: 119 us -> 106 us
  starting transfers between devices: 29.5 us -> 34.9 us
  matrix products: 56.8 us -> 61.1 us
  other arithmetic: 35 us -> 32.3 us
    all_gather x1 -> x2, waiting for transfers between devices: 31.3 us -> 14.7 us  [local(): lax.all_gather(part, 'col', axis=0, tiled=True, axis_index_groups=groups)]
    ppermute x1, starting transfers between devices: 9.88 us -> 18.9 us  [local(): lax.ppermute(flat, 'col', [(i, (i + 4 * step) % count) for i in range(cou...]
    ppermute x2, waiting for transfers between devices: 2.4 us -> 6.86 us  [extended(): lax.ppermute(head, axis, [((i + 1) % count, i) for i in range(ends)])]
    dot_general x4, matrix products: 10.5 us -> 13.3 us  [mlp(): return jnp.dot(hidden, weight_out, preferred_element_type=jnp.float32)]
  transfers between devices with their start and end apart: 13 -> 14, of which waited for: 6 -> 8; matrix products, arithmetic and copies ran while one was open for 33% -> 34% of each run, Pallas kernels for 0% -> 0%
where the time goes in v6:
time: 261 us
  waiting for transfers between devices  106 us (41%)
  matrix products  61.1 us (23%)
  starting transfers between devices  34.9 us (13%)
  other arithmetic  32.3 us (12%)
  between operations  13.7 us (5%)
  blocking collectives  9.62 us (4%)
    dot_general x4, matrix products, expand(): lax.dot_general(rows, weight_rows, (((1,), (1,)), ((), ())), preferred_el...  44.7 us
    ppermute x1, waiting for transfers between devices, local(): lax.ppermute(flat, 'col', [(i, (i + 4 * step) % count) for i in range(cou...  30.5 us
    all_to_all x1, waiting for transfers between devices, local(): lax.all_to_all(patches, 'col', split_axis=0, concat_axis=0, tiled=True)  27.9 us
    reduce_sum x1, other arithmetic, local(): mean = jnp.mean(conv, axis=-1, keepdims=True)  26.2 us
    ppermute x1, waiting for transfers between devices, local(): lax.ppermute(total, 'col', [((i + 4 * step) % count, i) for i in range(co...  22 us
    ppermute x1, starting transfers between devices, local(): lax.ppermute(flat, 'col', [(i, (i + 4 * step) % count) for i in range(cou...  18.9 us
    all_gather x2, waiting for transfers between devices, local(): lax.all_gather(part, 'col', axis=0, tiled=True, axis_index_groups=groups)  14.7 us
    dot_general x4, matrix products, mlp(): return jnp.dot(hidden, weight_out, preferred_element_type=jnp.float32)  13.3 us
  transfers between devices with their start and end apart: 14, of which 8 were waited for; matrix products, arithmetic and copies ran while one was open for 34% of the time, Pallas kernels for 0%

profile of v6, /device:TPU:0, one launch (start us, length us, event | category | flops | bytes accessed | tf_op | source)
XLA Modules:
  0.0 260.6 jit_solution(16555431279855938367)
XLA Ops:
  6.5 0.8 all_to_all.14
  7.3 9.6 %all_to_all.21 = s32[8,96,1]{1,2,0:T(1,128)S(1)} all-to-all(s32[8,96,1]{1,2,0:T(1,128)S(1)} %bitcast.35), channel_id=1, replica_groups=mesh['row'=4,'col'=8] {'col'}, dimensions={0} | all-to-all | bytes 6144 | tf_op jit(solution)/shard_map/all_to_all | solution.py:70
  16.9 4.4 %all-to-all-start.1 = ((bf16[8,96,1536]{2,1,0:T(8,128)(2,1)}), bf16[8,96,1536]{2,1,0:T(8,128)(2,1)}, u32[]{:S(2)}, u32[]{:S(2)}) async-start(bf16[8,96,1536]{2,1,0:T(8,128)(2,1)} %bitcast.29), calls=%async_computation.1 | async-start | bytes 4718592 | tf_op jit(solution)/shard_map/all_to_all | solution.py:69
  21.3 0.0 all-gather.3.cloned.1.call-start
  21.3 0.5 broadcast.323
  21.9 0.7 reduce.101
  22.5 0.1 eq.17
  22.6 0.3 fusion.45
  22.9 27.9 %all-to-all-done.1 = bf16[8,96,1536]{2,1,0:T(8,128)(2,1)} async-done(((bf16[8,96,1536]{2,1,0:T(8,128)(2,1)}), bf16[8,96,1536]{2,1,0:T(8,128)(2,1)}, u32[]{:S(2)}, u32[]{:S(2)}) %all-to-all-start.1) | async-done | bytes 2359328 | tf_op jit(solution)/shard_map/all_to_all | solution.py:69
  50.8 3.0 %fusion.40 = bf16[512,1536]{1,0:T(8,128)(2,1)S(1)} fusion(bf16[768,1536]{1,0:T(8,128)(2,1)} %bitcast.2, bf16[1536]{0:T(1024)(128)(2,1)S(1)} %copy-done.9, pred[512]{0:T(512)(128)(4,1)S(1)} %fusion.45, s32[768]{0:T(1024)S(1)} %eq.17), kind=kOutput, calls=%fused_computation.86 | convolution fusion | flops 1209139200 | bytes 3938816 | tf_op jit(solution)/shard_map/dot_general | solution.py:74
  53.9 3.6 %collective-permute-start = (bf16[3,16,1536]{2,1,0:T(8,128)(2,1)S(1)}, bf16[3,16,1536]{2,1,0:T(8,128)(2,1)S(1)}, u32[]{:S(2)}, u32[]{:S(2)}) collective-permute-start(bf16[3,16,1536]{2,1,0:T(8,128)(2,1)S(1)} %bitcast.34), channel_id=1, source_target_pairs={{0,8},{8,16},{16,24},{1,9},{9,17},{17,25},{2,10},{10,18},{18,26},{... | collective-permute-start | bytes 442376 | tf_op jit(solution)/shard_map/ppermute | solution.py:18
  57.5 1.3 collective-permute-start.1
  58.8 0.0 all-gather.3.cloned.1.call-update
  58.8 0.0 all-gather.5.cloned.1.call-start
  58.9 1.3 collective-permute-done
  60.1 4.4 %collective-permute-done.1 = bf16[3,16,1536]{2,1,0:T(8,128)(2,1)S(1)} collective-permute-done((bf16[3,16,1536]{2,1,0:T(8,128)(2,1)S(1)}, bf16[3,16,1536]{2,1,0:T(8,128)(2,1)S(1)}, u32[]{:S(2)}, u32[]{:S(2)}) %collective-permute-start.1) | collective-permute-done | bytes 147488 | tf_op jit(solution)/shard_map/ppermute | solution.py:20
  64.5 0.4 pad_maximum_fusion.5
  64.9 1.3 collective-permute-start.2
  66.2 1.5 collective-permute-start.3
  67.7 0.2 slice_reduce_fusion.46
  67.9 0.3 slice_reduce_fusion.48
  68.2 0.3 slice_reduce_fusion.47
  68.6 2.5 collective-permute-done.3
  71.1 1.6 maximum_maximum_fusion
  72.7 26.2 %fusion.47 = (f32[32,16]{1,0:T(8,128)S(1)}, f32[32,16,1536]{2,1,0:T(8,128)S(1)}) fusion(f32[1536]{0:T(1024)S(1)} %get-tuple-element.56, bf16[38,19,1536]{2,1,0:T(8,128)(2,1)S(1)} %get-tuple-element.61, f32[1536]{0:T(1024)S(1)} %get-tuple-element.57, f32[1536]{0:T(1024)S(1)} %get-tuple-element.10, f32[1536]{0:T(1024)S(1)} %get-tuple-element.11, ...), kind=kLoop, calls=%fused_computation.165 | loop fusion | flops 121110016 | bytes 71383040 | tf_op jit(solution)/shard_map/reduce_sum | solution.py:89
  98.9 0.4 multiply_reduce_fusion
  99.4 0.2 copy-done.2
  99.6 0.6 add_convert_fusion.2
  100.2 18.9 %collective-permute-start.4 = (bf16[512,1536]{1,0:T(8,128)(2,1)S(1)}, bf16[512,1536]{1,0:T(8,128)(2,1)}, u32[]{:S(2)}, u32[]{:S(2)}) collective-permute-start(bf16[512,1536]{1,0:T(8,128)(2,1)S(1)} %bitcast.30), channel_id=1, source_target_pairs={{0,4},{1,5},{2,6},{3,7},{4,0},{5,1},{6,2},{7,3},{8,12},{9,13},{10,... | collective-permute-start | bytes 4718600 | tf_op jit(solution)/shard_map/ppermute | solution.py:97
  119.1 0.4 collective-permute-start.5
  119.6 3.2 %collective-permute-done.5 = bf16[768]{0:T(1024)(128)(2,1)S(1)} collective-permute-done((bf16[768]{0:T(1024)(128)(2,1)S(1)}, bf16[768]{0:T(1024)(128)(2,1)S(1)}, u32[]{:S(2)}, u32[]{:S(2)}) %collective-permute-start.5) | collective-permute-done | bytes 1568 | tf_op jit(solution)/shard_map/ppermute | solution.py:64
  122.8 0.4 collective-permute-start.8
  123.1 30.5 %collective-permute-done.4 = bf16[512,1536]{1,0:T(8,128)(2,1)} collective-permute-done((bf16[512,1536]{1,0:T(8,128)(2,1)S(1)}, bf16[512,1536]{1,0:T(8,128)(2,1)}, u32[]{:S(2)}, u32[]{:S(2)}) %collective-permute-start.4) | collective-permute-done | bytes 1572896 | tf_op jit(solution)/shard_map/ppermute | solution.py:97
  153.7 1.0 collective-permute-start.6
  154.6 12.4 %fusion.2 = bf16[512,1536]{1,0:T(8,128)(2,1)} fusion(bf16[512,1536]{1,0:T(8,128)(2,1)} %collective-permute-done.4, bf16[1536,1536]{1,0:T(8,128)(2,1)} %all-gather.3.cloned.1.call-done, f32[1536]{0:T(1024)S(1)} %maximum_convert_fusion), kind=kOutput, calls=%fused_computation.11 | convolution fusion | flops 2467823616 | bytes 7870464 | tf_op jit(solution)/shard_map/dot_general | solution.py:28
  167.0 11.7 %fusion.5 = bf16[512,1536]{1,0:T(8,128)(2,1)} fusion(bf16[512,1536]{1,0:T(8,128)(2,1)} %collective-permute-done.6, bf16[1536,1536]{1,0:T(8,128)(2,1)S(1)} %copy-done.7, f32[1536]{0:T(1024)S(1)} %maximum_convert_fusion), kind=kOutput, calls=%fused_computation.14 | convolution fusion | flops 2467823616 | bytes 7870464 | tf_op jit(solution)/shard_map/dot_general | solution.py:28
  178.7 14.7 %all-gather.5.cloned.1.call-done = bf16[1536,1536]{1,0:T(8,128)(2,1)} async-done(((bf16[768,1536]{1,0:T(8,128)(2,1)}), bf16[1536,1536]{1,0:T(8,128)(2,1)}) %all-gather.5.cloned.1.call-update) | async-done | bytes 4718608 | tf_op jit(solution)/shard_map/all_gather | solution.py:61
  193.3 5.6 %convolution_convert_fusion.1 = bf16[512,1536]{1,0:T(8,128)(2,1)S(1)} fusion(bf16[512,1536]{1,0:T(8,128)(2,1)} %fusion.5, bf16[1536,1536]{1,0:T(8,128)(2,1)} %all-gather.5.cloned.1.call-done), kind=kOutput, calls=%fused_computation.88 | convolution fusion | flops 2416705536 | bytes 7864320 | tf_op jit(solution)/shard_map/dot_general | solution.py:36
  198.9 0.1 collective-permute-start.7
  199.0 10.4 %fusion.11 = bf16[512,1536]{1,0:T(8,128)(2,1)S(1)} fusion(bf16[512,1536]{1,0:T(8,128)(2,1)} %collective-permute-done.8, bf16[1536,1536]{1,0:T(8,128)(2,1)S(1)} %copy-done.8, f32[1536]{0:T(1024)S(1)} %maximum_convert_fusion), kind=kOutput, calls=%fused_computation.20 | convolution fusion | flops 2467823616 | bytes 7870464 | tf_op jit(solution)/shard_map/dot_general | solution.py:28
  209.4 2.6 convolution_convert_fusion
  212.0 0.5 collective-permute-start.9
  212.5 2.6 add_convert_fusion.1
  215.1 1.5 collective-permute-start.10
  216.7 10.2 %fusion.8 = bf16[512,1536]{1,0:T(8,128)(2,1)S(1)} fusion(bf16[512,1536]{1,0:T(8,128)(2,1)S(1)} %bitcast.32, bf16[1536,1536]{1,0:T(8,128)(2,1)S(1)} %copy-done.8, f32[1536]{0:T(1024)S(1)} %maximum_convert_fusion), kind=kOutput, calls=%fused_computation.17 | convolution fusion | flops 2467823616 | bytes 7870464 | tf_op jit(solution)/shard_map/dot_general | solution.py:28
  227.0 2.6 fusion.49
  229.6 22.0 %collective-permute-done.10 = bf16[512,1536]{1,0:T(8,128)(2,1)S(1)} collective-permute-done((bf16[512,1536]{1,0:T(8,128)(2,1)S(1)}, bf16[512,1536]{1,0:T(8,128)(2,1)S(1)}, u32[]{:S(2)}, u32[]{:S(2)}) %collective-permute-start.10) | collective-permute-done | bytes 1572896 | tf_op jit(solution)/shard_map/ppermute | solution.py:107
  251.6 2.2 add_convert_fusion
  (38 shorter events, 0.2 us)
Async XLA Ops:
  6.5 44.2 %copy-start.9 = (bf16[1536]{0:T(1024)(128)(2,1)S(1)}, bf16[1536]{0:T(1024)(128)(2,1)}, u32[]{:S(2)}) copy-start(bf16[1536]{0:T(1024)(128)(2,1)} %param.14) | copy-start | bytes 9220
  16.9 33.8 %all-to-all-start.1 = ((bf16[8,96,1536]{2,1,0:T(8,128)(2,1)}), bf16[8,96,1536]{2,1,0:T(8,128)(2,1)}, u32[]{:S(2)}, u32[]{:S(2)}) async-start(bf16[8,96,1536]{2,1,0:T(8,128)(2,1)} %bitcast.29), calls=%async_computation.1 | async-start | bytes 4718592 | tf_op jit(solution)/shard_map/all_to_all | solution.py:69
  21.3 133.3 %all-gather.3.cloned.1.call-start = ((), (), s32[]{:S(2)}) async-start(), calls=%async_computation.2 | async-start | bytes 7077888 | tf_op jit(solution)/shard_map/all_gather | solution.py:61
  53.8 13.9 %copy-start = (f32[7,7,1536]{2,1,0:T(8,128)S(1)}, f32[7,7,1536]{2,1,0:T(8,128)}, u32[]{:S(2)}) copy-start(f32[7,7,1536]{2,1,0:T(8,128)} %param.15) | copy-start | bytes 903172
  53.9 6.3 %collective-permute-start = (bf16[3,16,1536]{2,1,0:T(8,128)(2,1)S(1)}, bf16[3,16,1536]{2,1,0:T(8,128)(2,1)S(1)}, u32[]{:S(2)}, u32[]{:S(2)}) collective-permute-start(bf16[3,16,1536]{2,1,0:T(8,128)(2,1)S(1)} %bitcast.34), channel_id=1, source_target_pairs={{0,8},{8,16},{16,24},{1,9},{9,17},{17,25},{2,10},{10,18},{18,26},{... | collective-permute-start | bytes 442376 | tf_op jit(solution)/shard_map/ppermute | solution.py:18
  57.5 7.0 %collective-permute-start.1 = (bf16[3,16,1536]{2,1,0:T(8,128)(2,1)S(1)}, bf16[3,16,1536]{2,1,0:T(8,128)(2,1)S(1)}, u32[]{:S(2)}, u32[]{:S(2)}) collective-permute-start(bf16[3,16,1536]{2,1,0:T(8,128)(2,1)S(1)} %bitcast.33), channel_id=1, source_target_pairs={{8,0},{16,8},{24,16},{9,1},{17,9},{25,17},{10,2},{18,10},{26,18},{... | collective-permute-start | bytes 442376 | tf_op jit(solution)/shard_map/ppermute | solution.py:20
  58.8 134.5 %all-gather.5.cloned.1.call-start = ((), (), s32[]{:S(2)}) async-start(), calls=%async_computation.3 | async-start | bytes 7077888 | tf_op jit(solution)/shard_map/all_gather | solution.py:61
  64.9 3.7 %collective-permute-start.2 = (bf16[38,3,1536]{2,1,0:T(4,128)(2,1)S(1)}, bf16[38,3,1536]{2,1,0:T(4,128)(2,1)S(1)}, u32[]{:S(2)}, u32[]{:S(2)}) collective-permute-start(bf16[38,3,1536]{2,1,0:T(4,128)(2,1)S(1)} %get-tuple-element.62), channel_id=1, source_target_pairs={{0,1},{1,2},{2,3},{3,4},{4,5},{5,6},{6,7},{8,9},{9,10},{10,11},{11... | collective-permute-start | bytes 1050632 | tf_op jit(solution)/shard_map/ppermute | solution.py:18
  66.2 4.8 %collective-permute-start.3 = (bf16[38,3,1536]{2,1,0:T(4,128)(2,1)S(1)}, bf16[38,3,1536]{2,1,0:T(4,128)(2,1)S(1)}, u32[]{:S(2)}, u32[]{:S(2)}) collective-permute-start(bf16[38,3,1536]{2,1,0:T(4,128)(2,1)S(1)} %get-tuple-element.63), channel_id=1, source_target_pairs={{1,0},{2,1},{3,2},{4,3},{5,4},{6,5},{7,6},{9,8},{10,9},{11,10},{12... | collective-permute-start | bytes 1050632 | tf_op jit(solution)/shard_map/ppermute | solution.py:20
  68.6 4.1 %copy-start.1 = (f32[1536]{0:T(1024)S(1)}, f32[1536]{0:T(1024)}, u32[]{:S(2)}) copy-start(f32[1536]{0:T(1024)} %param.16) | copy-start | bytes 18436
  98.9 0.7 copy-start.2
  98.9 0.7 copy-start.3
  99.4 19.8 %copy-start.6 = (bf16[768]{0:T(1024)(128)(2,1)S(1)}, bf16[768]{0:T(1024)(128)(2,1)}, u32[]{:S(2)}) copy-start(bf16[768]{0:T(1024)(128)(2,1)} %param.20) | copy-start | bytes 4612
  100.2 53.4 %collective-permute-start.4 = (bf16[512,1536]{1,0:T(8,128)(2,1)S(1)}, bf16[512,1536]{1,0:T(8,128)(2,1)}, u32[]{:S(2)}, u32[]{:S(2)}) collective-permute-start(bf16[512,1536]{1,0:T(8,128)(2,1)S(1)} %bitcast.30), channel_id=1, source_target_pairs={{0,4},{1,5},{2,6},{3,7},{4,0},{5,1},{6,2},{7,3},{8,12},{9,13},{10,... | collective-permute-start | bytes 4718600 | tf_op jit(solution)/shard_map/ppermute | solution.py:97
  119.1 3.6 %collective-permute-start.5 = (bf16[768]{0:T(1024)(128)(2,1)S(1)}, bf16[768]{0:T(1024)(128)(2,1)S(1)}, u32[]{:S(2)}, u32[]{:S(2)}) collective-permute-start(bf16[768]{0:T(1024)(128)(2,1)S(1)} %copy-done.6), channel_id=1, source_target_pairs={{0,2},{1,3},{2,0},{3,1},{4,6},{5,7},{6,4},{7,5},{8,10},{9,11},{10,... | collective-permute-start | bytes 4616 | tf_op jit(solution)/shard_map/ppermute | solution.py:64
  122.8 76.2 %collective-permute-start.8 = (bf16[512,1536]{1,0:T(8,128)(2,1)S(1)}, bf16[512,1536]{1,0:T(8,128)(2,1)}, u32[]{:S(2)}, u32[]{:S(2)}) collective-permute-start(bf16[512,1536]{1,0:T(8,128)(2,1)S(1)} %bitcast.31), channel_id=1, source_target_pairs={{0,1},{1,0},{2,3},{3,2},{4,5},{5,4},{6,7},{7,6},{8,9},{9,8},{10,11... | collective-permute-start | bytes 4718600 | tf_op jit(solution)/shard_map/ppermute | solution.py:94
  153.7 13.3 %collective-permute-start.6 = (bf16[512,1536]{1,0:T(8,128)(2,1)}, bf16[512,1536]{1,0:T(8,128)(2,1)}, u32[]{:S(2)}, u32[]{:S(2)}) collective-permute-start(bf16[512,1536]{1,0:T(8,128)(2,1)} %collective-permute-done.4), channel_id=1, source_target_pairs={{0,1},{1,0},{2,3},{3,2},{4,5},{5,4},{6,7},{7,6},{8,9},{9,8},{10,11... | collective-permute-start | bytes 4718600 | tf_op jit(solution)/shard_map/ppermute | solution.py:98
  154.6 12.4 %copy-start.7 = (bf16[1536,1536]{1,0:T(8,128)(2,1)S(1)}, bf16[1536,1536]{1,0:T(8,128)(2,1)}, u32[]{:S(2)}) copy-start(bf16[1536,1536]{1,0:T(8,128)(2,1)} %all-gather.3.cloned.1.call-done) | copy-start | bytes 14155780
  193.3 5.7 %copy-start.8 = (bf16[1536,1536]{1,0:T(8,128)(2,1)S(1)}, bf16[1536,1536]{1,0:T(8,128)(2,1)}, u32[]{:S(2)}) copy-start(bf16[1536,1536]{1,0:T(8,128)(2,1)} %all-gather.3.cloned.1.call-done) | copy-start | bytes 14155780
  193.3 16.1 %slice-start = ((s8[4718592]{0:T(1024)(128)(4,1)}), s8[4194304]{0:T(1024)(128)(4,1)S(1)}, s32[]{:S(2)}) async-start(s8[4718592]{0:T(1024)(128)(4,1)} %bitcast.36), calls=%async_computation.4 | async-start | bytes 8388608
  198.9 10.5 %slice-start.1 = ((s8[4718592]{0:T(1024)(128)(4,1)}), s8[524288]{0:T(1024)(128)(4,1)S(1)}, s32[]{:S(2)}) async-start(s8[4718592]{0:T(1024)(128)(4,1)} %bitcast.36), calls=%async_computation.5 | async-start | bytes 1048576
  198.9 13.6 %collective-permute-start.7 = (bf16[512,1536]{1,0:T(8,128)(2,1)S(1)}, bf16[512,1536]{1,0:T(8,128)(2,1)S(1)}, u32[]{:S(2)}, u32[]{:S(2)}) collective-permute-start(bf16[512,1536]{1,0:T(8,128)(2,1)S(1)} %convolution_convert_fusion.1), channel_id=1, source_target_pairs={{0,1},{1,0},{2,3},{3,2},{4,5},{5,4},{6,7},{7,6},{8,9},{9,8},{10,11... | collective-permute-start | bytes 4718600 | tf_op jit(solution)/shard_map/ppermute | solution.py:103
  209.4 3.1 %copy-start.10 = (bf16[512,1536]{1,0:T(8,128)(2,1)S(1)}, bf16[512,1536]{1,0:T(8,128)(2,1)}, u32[]{:S(2)}) copy-start(bf16[512,1536]{1,0:T(8,128)(2,1)} %fusion.2) | copy-start | bytes 4718596
  212.0 17.5 %collective-permute-start.9 = (bf16[512,1536]{1,0:T(8,128)(2,1)S(1)}, bf16[512,1536]{1,0:T(8,128)(2,1)S(1)}, u32[]{:S(2)}, u32[]{:S(2)}) collective-permute-start(bf16[512,1536]{1,0:T(8,128)(2,1)S(1)} %convolution_convert_fusion), channel_id=1, source_target_pairs={{0,1},{1,0},{2,3},{3,2},{4,5},{5,4},{6,7},{7,6},{8,9},{9,8},{10,11... | collective-permute-start | bytes 4718600 | tf_op jit(solution)/shard_map/ppermute | solution.py:113
  215.1 36.4 %collective-permute-start.10 = (bf16[512,1536]{1,0:T(8,128)(2,1)S(1)}, bf16[512,1536]{1,0:T(8,128)(2,1)S(1)}, u32[]{:S(2)}, u32[]{:S(2)}) collective-permute-start(bf16[512,1536]{1,0:T(8,128)(2,1)S(1)} %add_convert_fusion.1), channel_id=1, source_target_pairs={{4,0},{5,1},{6,2},{7,3},{0,4},{1,5},{2,6},{3,7},{12,8},{13,9},{14,... | collective-permute-start | bytes 4718600 | tf_op jit(solution)/shard_map/ppermute | solution.py:107
  226.9 24.7 %copy-start.4 = (f32[1536]{0:T(1024)S(1)}, f32[1536]{0:T(1024)}, u32[]{:S(2)}) copy-start(f32[1536]{0:T(1024)} %param.22) | copy-start | bytes 18436
  226.9 24.6 %copy-start.5 = (f32[1536]{0:T(1024)S(1)}, f32[1536]{0:T(1024)}, u32[]{:S(2)}) copy-start(f32[1536]{0:T(1024)} %param.23) | copy-start | bytes 18436
Sparse Core Ops, SparseCore 0:
  58.9 71.6 all-gather.2
  132.2 61.1 all-gather.4
